TPU v7x, 32 devices: a whole 2x2x4 slice. The times are simulated.
32 devices in a mesh: section: 4 (over x, core), dp: 4 (over z), mp: 2 (over y).
Axes of the slice: x: 2, y: 2, z: 4, core: 2. Of those that a mesh axis runs over, the one named last changes fastest.
Arguments:
- siglip_features: bfloat16 [2048, 1152], P('dp'), may hold values from -6 to 6
- convnext_features: bfloat16 [2048, 1536], P('dp'), may hold values from -6 to 6
- siglip_projection: bfloat16 [1152, 8192], P(None, ('section', 'mp')), may hold values from -0.125 to 0.125
- convnext_projection: bfloat16 [1536, 8192], P(None, ('section', 'mp')), may hold values from -0.125 to 0.125
- newline_embed: bfloat16 [8192], P(('section', 'mp')), may hold values from -6 to 6
- key_value_weight: bfloat16 [2048, 8192], P(None, ('section', 'mp')), may hold values from -0.0625 to 0.0625
- tile_rank: int32 [64, 1], replicated, may hold values from 0 to 3; in each aligned block of 16 rows (0 to 15, 16 to 31, ...) at most 8 rows name the same one
- row_end: int32 [64], replicated, may hold values 0 or 1
- key_value_grad: bfloat16 [4096, 2048], P('dp'), may hold values from -0.059814453 to 0.059814453
- newline_grad: bfloat16 [128, 2048], P('dp'), may hold values from -1.796875 to 1.796875
Outputs:
- siglip_weight_grad: float32 [1152, 8192], P('dp', ('section', 'mp'))
- convnext_weight_grad: float32 [1536, 8192], P('dp', ('section', 'mp'))
- key_value_weight_grad: float32 [2048, 8192], P('dp', ('section', 'mp'))
Inputs may be any that keep to these rules, and one draw needn't show every extreme that they name: `tile_rank`: each aligned block of 16 tiles (the tiles of one index of dp) sends at most 8 tiles to one rank, and exactly 8 to some rank.
All inputs are finite; a program needn't handle non-finite values.
Results may differ from a plain program's by a relative error of at most 0.007.
Values may be sent and summed in bfloat16 or wider, within the bound.
A program may use at most 128 MiB of HBM per device.

v0:
```python
import jax
import jax.numpy as jnp
from jax import lax
from jax.sharding import PartitionSpec as P

D = 8192


epsilon = 1e-06


def tile_places(tile_rank, groups):
    dest_rank = tile_rank[:, 0]
    tile_count = dest_rank.shape[0]
    per_device = tile_count // groups
    onehot = (dest_rank[:, None] == jnp.arange(groups, dtype=jnp.int32)[None, :]).astype(jnp.int32)
    blocks = onehot.reshape(groups, per_device, groups)
    before = jnp.cumsum(blocks, axis=1) - blocks
    slot_place = jnp.sum(before * blocks, axis=2).reshape(tile_count)
    source = jnp.arange(tile_count, dtype=jnp.int32) // per_device
    return (dest_rank, source, slot_place)


def row_norms(squares):
    return lax.psum((squares[0], squares[1]), ("section", "mp"))


def row_products(products):
    return lax.psum(products, ("section", "mp"))


def norm_backward(inverse_rms, grad_values, proj_values):
    products = row_products(jnp.sum(grad_values * proj_values, axis=1))[:, None]
    return (inverse_rms * grad_values - inverse_rms**3 * proj_values * products / D).astype(
        jnp.bfloat16
    )


def local(
    siglip_features,
    convnext_features,
    siglip_projection,
    convnext_projection,
    newline_embed,
    key_value_weight,
    tile_rank,
    row_end,
    key_value_grad,
    newline_grad,
):
    groups = lax.axis_size("dp")
    my_rank = lax.axis_index("dp")
    dest_rank, source, slot_place = tile_places(tile_rank, groups)
    per_device = dest_rank.shape[0] // groups
    capacity = 2 * per_device // groups
    row_count = siglip_features.shape[0]
    tile_rows = row_count // per_device
    share = siglip_projection.shape[1]
    mine_dest = lax.dynamic_slice_in_dim(dest_rank, my_rank * per_device, per_device)
    mine_place = lax.dynamic_slice_in_dim(slot_place, my_rank * per_device, per_device)
    rank_ids = jnp.arange(groups, dtype=jnp.int32)[:, None, None]
    place_ids = jnp.arange(capacity, dtype=jnp.int32)[None, :, None]
    select = (
        (mine_dest[None, None, :] == rank_ids) & (mine_place[None, None, :] == place_ids)
    ).astype(jnp.bfloat16)
    projected = (
        jnp.dot(siglip_features, siglip_projection, preferred_element_type=jnp.float32)
        + jnp.dot(convnext_features, convnext_projection, preferred_element_type=jnp.float32)
    ).astype(jnp.bfloat16)
    line_vector = newline_embed.astype(jnp.float32)
    line_square = jnp.sum(line_vector * line_vector)
    outgoing = jnp.einsum(
        "gcj,jtx->gctx",
        select,
        projected.reshape(per_device, tile_rows, share),
        preferred_element_type=jnp.float32,
    ).astype(jnp.bfloat16)
    outgoing = outgoing.reshape(groups, capacity * tile_rows, share)
    received = lax.all_to_all(outgoing, "dp", split_axis=0, concat_axis=0, tiled=True).reshape(
        groups * capacity * tile_rows, share
    )
    recv_values = received.astype(jnp.float32)
    statistic = row_norms((jnp.sum(recv_values * recv_values, axis=1), line_square))
    recv_inverse = lax.rsqrt(statistic[0] / D + epsilon)[:, None]
    line_total_sq = statistic[1]
    normed = (recv_values * recv_inverse).astype(jnp.bfloat16)
    line_normed = (line_vector * lax.rsqrt(line_total_sq / D + epsilon)).astype(jnp.bfloat16)
    slot_global = source * capacity + slot_place
    line_live = (dest_rank == my_rank) & (row_end == 1)
    slot_ids = jnp.arange(groups * capacity, dtype=jnp.int32)[None, :]
    newline_mask = jnp.sum(
        ((slot_global[:, None] == slot_ids) & line_live[:, None]).astype(jnp.int32), axis=0
    )
    line_total = jnp.dot(
        newline_mask.astype(jnp.bfloat16)[None, :], newline_grad, preferred_element_type=jnp.float32
    )[0]
    kv_term = lax.dot_general(
        key_value_grad, normed, (((0,), (0,)), ((), ())), preferred_element_type=jnp.float32
    )
    kv_term = kv_term + line_total[:, None] * line_normed.astype(jnp.float32)[None, :]
    normed_grad = jnp.dot(
        key_value_grad, key_value_weight, preferred_element_type=jnp.float32
    ).astype(jnp.bfloat16)
    returning = norm_backward(recv_inverse, normed_grad.astype(jnp.float32), recv_values)
    returned = lax.all_to_all(
        returning.reshape(groups, capacity * tile_rows, share),
        "dp",
        split_axis=0,
        concat_axis=0,
        tiled=True,
    )
    tile_back = jnp.einsum(
        "gcj,gctx->jtx",
        select,
        returned.reshape(groups, capacity, tile_rows, share),
        preferred_element_type=jnp.float32,
    ).reshape(row_count, share)
    projected_grad = tile_back.astype(jnp.bfloat16)
    contract = (((0,), (0,)), ((), ()))
    siglip_term = lax.dot_general(
        siglip_features, projected_grad, contract, preferred_element_type=jnp.float32
    )
    convnext_term = lax.dot_general(
        convnext_features, projected_grad, contract, preferred_element_type=jnp.float32
    )
    siglip_result, convnext_result, kv_result = (
        lax.psum_scatter(siglip_term, "dp", scatter_dimension=0, tiled=True),
        lax.psum_scatter(convnext_term, "dp", scatter_dimension=0, tiled=True),
        lax.psum_scatter(kv_term, "dp", scatter_dimension=0, tiled=True),
    )
    return (siglip_result, convnext_result, kv_result)


def solution(mesh):
    in_specs = (
        P("dp", None),
        P("dp", None),
        P(None, ("section", "mp")),
        P(None, ("section", "mp")),
        P(("section", "mp")),
        P(None, ("section", "mp")),
        P(),
        P(),
        P("dp", None),
        P("dp", None),
    )
    out_specs = (P("dp", ("section", "mp")), P("dp", ("section", "mp")), P("dp", ("section", "mp")))
    return jax.shard_map(local, mesh=mesh, in_specs=in_specs, out_specs=out_specs, check_vma=False)
```

profile of v0, /device:TPU:0, one launch (start us, length us, event | category | flops | bytes accessed | tf_op | source)
XLA Modules:
  0.0 512.9 jit_solution(3964856764752096273)
XLA Ops:
  7.2 0.0 copy-start
  7.2 0.5 broadcast.90
  7.7 1.6 reduce.4
  9.3 0.1 eq.84
  9.4 0.1 fusion.13
  9.5 0.2 select_reduce_fusion
  9.7 0.1 reshape.120
  9.8 0.7 dynamic-slice_bitcast_fusion
  10.5 0.1 dynamic_slice.7
  10.6 3.7 fusion.27
  14.3 0.0 copy-done
  14.3 0.0 copy-done.8
  14.3 1.8 add_convert_fusion
  16.1 0.9 convolution_convert_fusion.1
  17.0 2.5 copy.32
  19.5 6.5 %all-to-all-start = ((bf16[4,256,1024]{2,1,0:T(8,128)(2,1)}), bf16[4,256,1024]{2,1,0:T(8,128)(2,1)S(1)}, u32[]{:S(2)}, u32[]{:S(2)}) async-start(bf16[4,256,1024]{2,1,0:T(8,128)(2,1)} %bitcast.62), calls=%async_computation | async-start | bytes 4194304 | tf_op jit(solution)/shard_map/all_to_all | solution.py:79
  25.9 0.0 reduce-scatter.6.cloned.1.call-start
  25.9 0.0 copy-done.5
  25.9 0.6 fusion.19
  26.5 47.6 %all-to-all-done = bf16[4,256,1024]{2,1,0:T(8,128)(2,1)S(1)} async-done(((bf16[4,256,1024]{2,1,0:T(8,128)(2,1)}), bf16[4,256,1024]{2,1,0:T(8,128)(2,1)S(1)}, u32[]{:S(2)}, u32[]{:S(2)}) %all-to-all-start) | async-done | bytes 2097184 | tf_op jit(solution)/shard_map/all_to_all | solution.py:79
  74.1 0.5 fusion.3
  74.6 9.3 %fusion.2 = (f32[1024]{0:T(1024)S(1)}, bf16[1024,1024]{1,0:T(8,128)(2,1)}) fusion(bf16[4,256,1024]{2,1,0:T(8,128)(2,1)S(1)} %all-to-all-done, bf16[1024,2048]{1,0:T(8,128)(2,1)} %param.18, bf16[2048,1024]{1,0:T(8,128)(2,1)} %param.15), kind=kOutput, calls=%fused_computation.7 | convolution fusion | flops 4300209152 | bytes 12587008 | tf_op jit(solution)/shard_map/dot_general | solution.py:101
  83.9 14.9 %all-reduce = (f32[1024]{0:T(1024)S(1)}, f32[1024]{0:T(1024)S(1)}, f32[]{:T(128)}) all-reduce(f32[1024]{0:T(1024)S(1)} %get-tuple-element.22, f32[1024]{0:T(1024)S(1)} %bitcast.68, f32[]{:T(128)} %fusion.19), channel_id=1, replica_groups=mesh['section'=4,'dp'=4,'mp'=2] {'section','mp'}, use_global_device_ids=true, to_apply=%region_5.6 | all-reduce | flops 2049 | bytes 16392 | tf_op jit(solution)/shard_map/psum | solution.py:29
  98.8 3.7 fusion.6
  102.5 51.1 %all_to_all.10 = bf16[4,256,1024]{2,1,0:T(8,128)(2,1)S(1)} all-to-all(bf16[4,256,1024]{2,1,0:T(8,128)(2,1)S(1)} %bitcast.61), channel_id=1, replica_groups=mesh['section'=4,'dp'=4,'mp'=2] {'dp'}, dimensions={0} | all-to-all | bytes 4194304 | tf_op jit(solution)/shard_map/all_to_all | solution.py:105
  153.6 2.3 bitcast_convert_fusion
  155.9 0.6 copy.34
  156.5 0.0 copy-done.9
  156.5 4.5 convolution_bitcast_fusion
  161.1 0.0 reduce-scatter.6.cloned.1.call-update
  161.1 0.0 reduce-scatter.8.cloned.1.call-start
  161.2 0.6 copy-done.6
  161.7 0.0 copy-done.7
  161.8 0.1 convert_reduce_fusion
  161.9 0.1 copy-done.4
  162.0 0.1 fusion.24
  162.9 9.0 %bitcast_add_fusion = f32[2048,1024]{0,1:T(8,128)} fusion(bf16[1024,1024]{1,0:T(8,128)(2,1)S(1)} %copy-done.2, bf16[1024,2048]{1,0:T(8,128)(2,1)} %param.18, f32[1024]{0:T(1024)S(1)} %fusion.21, f32[2048]{0:T(1024)S(1)} %bitcast.69), kind=kOutput, calls=%fused_computation | convolution fusion | flops 4299161600 | bytes 14692352 | tf_op jit(solution)/shard_map/dot_general | solution.py:97
  171.9 0.0 reduce-scatter.8.cloned.1.call-update
  171.9 0.0 reduce-scatter.10.cloned.1.call-start
  172.0 1.2 copy-done.3
  173.2 3.7 convolution_bitcast_fusion.1
  176.9 6.2 %copy.40 = f32[1152,1024]{1,0:T(8,128)} copy(f32[1152,1024]{0,1:T(8,128)} %convolution_bitcast_fusion.1) | data formatting | bytes 9437184
  183.1 0.0 reduce-scatter.10.cloned.1.call-update
  183.1 87.0 %reduce-scatter.6.cloned.1.call-done = f32[384,1024]{0,1:T(8,128)} async-done(((f32[1536,1024]{0,1:T(8,128)}), f32[384,1024]{0,1:T(8,128)}) %reduce-scatter.6.cloned.1.call-update) | async-done | bytes 1572880 | tf_op jit(solution)/shard_map/reduce_scatter | solution.py:128
  270.1 3.2 copy.36
  273.3 144.2 %reduce-scatter.8.cloned.1.call-done = f32[512,1024]{0,1:T(8,128)} async-done(((f32[2048,1024]{0,1:T(8,128)}), f32[512,1024]{0,1:T(8,128)}) %reduce-scatter.8.cloned.1.call-update) | async-done | bytes 2097168 | tf_op jit(solution)/shard_map/reduce_scatter | solution.py:129
  417.5 2.9 copy.37
  420.4 86.0 %reduce-scatter.10.cloned.1.call-done = f32[288,1024]{1,0:T(8,128)} async-done(((f32[1152,1024]{1,0:T(8,128)}), f32[288,1024]{1,0:T(8,128)}) %reduce-scatter.10.cloned.1.call-update) | async-done | bytes 1179664
  (19 shorter events, 0.1 us)
Async XLA Ops:
  7.2 7.1 %copy-start = (bf16[1536,1024]{1,0:T(8,128)(2,1)S(1)}, bf16[1536,1024]{1,0:T(8,128)(2,1)}, u32[]{:S(2)}) copy-start(bf16[1536,1024]{1,0:T(8,128)(2,1)} %param.13) | copy-start | bytes 9437188
  10.6 3.7 copy-start.8
  19.5 6.5 %copy-start.5 = (bf16[1024]{0:T(1024)(128)(2,1)S(1)}, bf16[1024]{0:T(1024)(128)(2,1)}, u32[]{:S(2)}) copy-start(bf16[1024]{0:T(1024)(128)(2,1)} %param.14) | copy-start | bytes 6148
  19.5 54.6 %all-to-all-start = ((bf16[4,256,1024]{2,1,0:T(8,128)(2,1)}), bf16[4,256,1024]{2,1,0:T(8,128)(2,1)S(1)}, u32[]{:S(2)}, u32[]{:S(2)}) async-start(bf16[4,256,1024]{2,1,0:T(8,128)(2,1)} %bitcast.62), calls=%async_computation | async-start | bytes 4194304 | tf_op jit(solution)/shard_map/all_to_all | solution.py:79
  25.9 244.2 %reduce-scatter.6.cloned.1.call-start = ((), (), s32[]{:S(2)}) async-start(), calls=%async_computation.5 | async-start | bytes 7864320 | tf_op jit(solution)/shard_map/reduce_scatter | solution.py:128
  153.6 2.9 copy-start.9
  161.1 0.7 copy-start.6
  161.1 0.7 copy-start.7
  161.1 0.9 copy-start.4
  161.1 1.8 copy-start.2
  161.1 256.4 %reduce-scatter.8.cloned.1.call-start = ((), (), s32[]{:S(2)}) async-start(), calls=%async_computation.6 | async-start | bytes 10485760 | tf_op jit(solution)/shard_map/reduce_scatter | solution.py:129
  171.9 1.3 copy-start.3
  171.9 334.5 %reduce-scatter.10.cloned.1.call-start = ((), (), s32[]{:S(2)}) async-start(), calls=%async_computation.7 | async-start | bytes 5898240
  270.1 236.3 %copy-start.1 = (bf16[1536,1024]{1,0:T(8,128)(2,1)S(1)}, bf16[1536,1024]{1,0:T(8,128)(2,1)}, u32[]{:S(2)}) copy-start(bf16[1536,1024]{1,0:T(8,128)(2,1)} %param.13) | copy-start | bytes 9437188
Sparse Core Ops, SparseCore 0:
  161.2 108.8 reduce-scatter.5
  272.5 144.9 reduce-scatter.7
  420.4 85.9 reduce-scatter.9
where the time goes:
time: 513 us
  waiting for transfers between devices  365 us (71%)
  blocking collectives  66 us (13%)
  matrix products  35.4 us (7%)
  local copies, waits for them, and re-layouts  18.7 us (4%)
  between operations  14.5 us (3%)
  other arithmetic  6.84 us (1%)
  starting transfers between devices  6.54 us (1%)
    reduce_scatter x1, waiting for transfers between devices, local(): lax.psum_scatter(kv_term, 'dp', scatter_dimension=0, tiled=True)  144 us
    reduce_scatter x1, waiting for transfers between devices, local(): lax.psum_scatter(convnext_term, 'dp', scatter_dimension=0, tiled=True)  87 us
    unnamed x4, waiting for transfers between devices  86.1 us
    all_to_all x1, blocking collectives, local(): lax.all_to_all(returning.reshape(groups, capacity * tile_rows, share), 'd...  51.1 us
    all_to_all x1, waiting for transfers between devices, local(): lax.all_to_all(outgoing, 'dp', split_axis=0, concat_axis=0, tiled=True)  47.6 us
    psum x1, blocking collectives, row_products(): return lax.psum(products, ('section', 'mp'))  14.9 us
    unnamed x25, local copies, waits for them, and re-layouts  14.7 us
  transfers between devices with their start and end apart: 4, of which 4 were waited for; matrix products, arithmetic and copies ran while one was open for 5% of the time, Pallas kernels for 0%

commit v1 on v0

--- a/solution.py
+++ b/solution.py
@@ -36,7 +36,7 @@
     )
 
 
-def local(
+def local_reducing(
     siglip_features,
     convnext_features,
     siglip_projection,
@@ -131,6 +131,109 @@
     return (siglip_result, convnext_result, kv_result)
 
 
+def local_gathering(
+    siglip_features,
+    convnext_features,
+    siglip_projection,
+    convnext_projection,
+    newline_embed,
+    key_value_weight,
+    tile_rank,
+    row_end,
+    key_value_grad,
+    newline_grad,
+):
+    groups = lax.axis_size("dp")
+    mates = lax.axis_size("section") * lax.axis_size("mp")
+    my_rank = lax.axis_index("dp")
+    me = lax.axis_index("section") * lax.axis_size("mp") + lax.axis_index("mp")
+    dest_rank, source, slot_place = tile_places(tile_rank, groups)
+    per_device = dest_rank.shape[0] // groups
+    capacity = 2 * per_device // groups
+    row_count, sig = siglip_features.shape
+    conv = convnext_features.shape[1]
+    tile_rows = row_count // per_device
+    part = tile_rows // mates
+    kv = key_value_grad.shape[1]
+    everyone = ("dp", "section", "mp")
+
+    def my_rows(x, tiles):
+        x = x.reshape(tiles, tile_rows, x.shape[1])
+        return lax.dynamic_slice_in_dim(x, me * part, part, axis=1)
+
+    features = jnp.concatenate([siglip_features, convnext_features], axis=1)
+    features = my_rows(features, per_device).reshape(per_device * part, sig + conv)
+    features = lax.all_gather(features, everyone, axis=0, tiled=True)
+
+    slots = my_rows(key_value_grad, groups * capacity).reshape(groups, capacity * part * kv)
+    slots = lax.all_to_all(slots, "dp", split_axis=0, concat_axis=0, tiled=True)
+    mine_dest = lax.dynamic_slice_in_dim(dest_rank, my_rank * per_device, per_device)
+    mine_place = lax.dynamic_slice_in_dim(slot_place, my_rank * per_device, per_device)
+    wanted = mine_dest * capacity + mine_place
+    select = (wanted[:, None] == jnp.arange(groups * capacity, dtype=jnp.int32)[None, :]).astype(
+        jnp.bfloat16
+    )
+    grads = jnp.dot(
+        select, slots.reshape(groups * capacity, part * kv), preferred_element_type=jnp.float32
+    ).astype(jnp.bfloat16)
+    grads = lax.all_gather(grads.reshape(per_device * part, kv), everyone, axis=0, tiled=True)
+
+    slot_global = source * capacity + slot_place
+    line_live = (dest_rank == my_rank) & (row_end == 1)
+    slot_ids = jnp.arange(groups * capacity, dtype=jnp.int32)[None, :]
+    newline_mask = jnp.sum(
+        ((slot_global[:, None] == slot_ids) & line_live[:, None]).astype(jnp.int32), axis=0
+    )
+    line_total = jnp.dot(
+        newline_mask.astype(jnp.bfloat16)[None, :], newline_grad, preferred_element_type=jnp.float32
+    )[0]
+    line_total = lax.psum_scatter(line_total, "dp", scatter_dimension=0, tiled=True)
+    line_vector = newline_embed.astype(jnp.float32)
+    line_square = jnp.sum(line_vector * line_vector)
+
+    projected = (
+        jnp.dot(features[:, :sig], siglip_projection, preferred_element_type=jnp.float32)
+        + jnp.dot(features[:, sig:], convnext_projection, preferred_element_type=jnp.float32)
+    ).astype(jnp.bfloat16)
+    proj_values = projected.astype(jnp.float32)
+    normed_grad = jnp.dot(grads, key_value_weight, preferred_element_type=jnp.float32).astype(
+        jnp.bfloat16
+    )
+    grad_values = normed_grad.astype(jnp.float32)
+    squares = jnp.sum(proj_values * proj_values, axis=1)
+    products = jnp.sum(grad_values * proj_values, axis=1)
+    squares, products, line_square = lax.psum((squares, products, line_square), ("section", "mp"))
+    inverse = lax.rsqrt(squares / D + epsilon)[:, None]
+    normed = (proj_values * inverse).astype(jnp.bfloat16)
+    line_normed = (line_vector * lax.rsqrt(line_square / D + epsilon)).astype(jnp.bfloat16)
+    projected_grad = (
+        inverse * grad_values - inverse**3 * proj_values * products[:, None] / D
+    ).astype(jnp.bfloat16)
+
+    def block(x, first, width):
+        return lax.dynamic_slice_in_dim(x, first + my_rank * (width // groups), width // groups, 1)
+
+    def contract(a, b):
+        return lax.dot_general(a, b, (((0,), (0,)), ((), ())), preferred_element_type=jnp.float32)
+
+    siglip_result = contract(block(features, 0, sig), projected_grad)
+    convnext_result = contract(block(features, sig, conv), projected_grad)
+    kv_result = contract(block(grads, 0, kv), normed)
+    kv_result = kv_result + line_total[:, None] * line_normed.astype(jnp.float32)[None, :]
+    return (siglip_result, convnext_result, kv_result)
+
+
+GATHER_LIMIT = 40 * 2**20
+
+
+def local(*args):
+    rows = lax.axis_size("dp") * args[0].shape[0]
+    width = args[0].shape[1] + args[1].shape[1] + args[8].shape[1]
+    if 2 * rows * width <= GATHER_LIMIT:
+        return local_gathering(*args)
+    return local_reducing(*args)
+
+
 def solution(mesh):
     in_specs = (
         P("dp", None),

time: 513 us -> 301 us (0.59)
  waiting for transfers between devices: 365 us -> 150 us
  blocking collectives: 66 us -> 35.3 us
  matrix products: 35.4 us -> 59.6 us
  other arithmetic: 6.84 us -> 15 us
    reduce_scatter x2 -> x0, waiting for transfers between devices: 231 us -> none  [the longest x1 144 us: local(): lax.psum_scatter(kv_term, 'dp', scatter_dimension=0, tiled=True)]
    all_gather x0 -> x2, waiting for transfers between devices: none -> 138 us  [the longest x1 77.3 us: local_gathering(): features = lax.all_gather(features, everyone, axis=0, tiled=True)]
    unnamed x4 -> x2, waiting for transfers between devices: 86.1 us -> 0.03 us
    all_to_all x1 -> x0, blocking collectives: 51.1 us -> none  [local(): lax.all_to_all(returning.reshape(groups, capacity * tile_rows, share), 'd...]
    all_to_all x1, waiting for transfers between devices: 47.6 us -> 12.8 us  [local_gathering(): slots = lax.all_to_all(slots, 'dp', split_axis=0, concat_axis=0, tiled=True)]
    dot_general x9 -> x8, matrix products: 35.4 us -> 59.6 us  [the longest x3 19.1 us: contract(): lax.dot_general(a, b, (((0,), (0,)), ((), ())), preferred_element_type=jn...]
    all_to_all x0 -> x2, other arithmetic: none -> 11.2 us  [local_gathering(): slots = lax.all_to_all(slots, 'dp', split_axis=0, concat_axis=0, tiled=True)]
    unnamed x0 -> x1, blocking collectives: none -> 10.3 us
  transfers between devices with their start and end apart: 4 -> 3, of which waited for: 4 -> 3; matrix products, arithmetic and copies ran while one was open for 5% -> 7% of each run, Pallas kernels for 0% -> 0%
where the time goes in v1:
time: 301 us; the launch traced here: 300 us
  waiting for transfers between devices  150 us (50%)
  matrix products  59.6 us (20%)
  blocking collectives  35.3 us (12%)
  local copies, waits for them, and re-layouts  18 us (6%)
  between operations  15.5 us (5%)
  other arithmetic  15 us (5%)
  starting transfers between devices  6.36 us (2%)
    all_gather x1, waiting for transfers between devices, local_gathering(): features = lax.all_gather(features, everyone, axis=0, tiled=True)  77.3 us
    all_gather x1, waiting for transfers between devices, local_gathering(): lax.all_gather(grads.reshape(per_device * part, kv), everyone, axis=0, ti...  60.2 us
    psum x1, blocking collectives, local_gathering(): lax.psum((squares, products, line_square), ('section', 'mp'))  25 us
    dot_general x3, matrix products, contract(): lax.dot_general(a, b, (((0,), (0,)), ((), ())), preferred_element_type=jn...  19.1 us
    dot_general x1, matrix products, local_gathering(): jnp.dot(grads, key_value_weight, preferred_element_type=jnp.float32)  14 us
    dot_general x1, matrix products, local_gathering(): jnp.dot(features[:, sig:], convnext_projection, preferred_element_type=jn...  13.7 us
    all_to_all x1, waiting for transfers between devices, local_gathering(): slots = lax.all_to_all(slots, 'dp', split_axis=0, concat_axis=0, tiled=True)  12.8 us
    all_to_all x2, other arithmetic, local_gathering(): slots = lax.all_to_all(slots, 'dp', split_axis=0, concat_axis=0, tiled=True)  11.2 us
  transfers between devices with their start and end apart: 3, of which 3 were waited for; matrix products, arithmetic and copies ran while one was open for 7% of the time, Pallas kernels for 0%

profile of v1, /device:TPU:0, one launch (start us, length us, event | category | flops | bytes accessed | tf_op | source)
XLA Modules:
  0.0 300.1 jit_solution(300543638943091713)
XLA Ops:
  7.2 0.0 copy-start
  7.2 0.0 copy-start.3
  7.2 2.5 constant_dynamic-slice_fusion
  9.7 3.6 %all_to_all.8 = bf16[4,1,65536]{2,1,0:T(2,128)(2,1)} reshape(bf16[32,4,2048]{2,1,0:T(4,128)(2,1)} %constant_dynamic-slice_fusion) | data formatting | bytes 1048576 | tf_op jit(solution)/shard_map/all_to_all | solution.py:169
  13.3 0.5 broadcast.70
  13.8 5.9 %reduce.5 = bf16[4,65536]{1,0:T(4,128)(2,1)} reduce(bf16[4,1,65536]{2,1,0:T(2,128)(2,1)} %all_to_all.8, bf16[]{:T(256)} %broadcast.70), dimensions={1}, to_apply=%all_to_all.8.reduce_sub_computation | reduce | bytes 1048578 | tf_op jit(solution)/shard_map/all_to_all | solution.py:169
  19.7 2.4 reshape.94
  22.1 6.3 %all-to-all-start = ((bf16[4,2,32768]{2,1,0:T(2,128)(2,1)}), bf16[4,2,32768]{2,1,0:T(2,128)(2,1)}, u32[]{:S(2)}, u32[]{:S(2)}) async-start(bf16[4,2,32768]{2,1,0:T(2,128)(2,1)} %reshape.94), calls=%async_computation | async-start | bytes 1048576 | tf_op jit(solution)/shard_map/all_to_all | solution.py:169
  28.4 0.0 all-gather.5.cloned.1.call-start
  28.4 0.5 broadcast.69
  28.9 0.0 copy-done.3
  28.9 0.7 reduce.4
  29.6 0.1 eq.55
  29.7 0.1 fusion.25
  29.8 0.2 select_reduce_fusion
  30.0 0.1 reshape.77
  30.1 0.1 fusion.38
  30.2 12.8 %all-to-all-done = bf16[4,2,32768]{2,1,0:T(2,128)(2,1)} async-done(((bf16[4,2,32768]{2,1,0:T(2,128)(2,1)}), bf16[4,2,32768]{2,1,0:T(2,128)(2,1)}, u32[]{:S(2)}, u32[]{:S(2)}) %all-to-all-start) | async-done | bytes 524320 | tf_op jit(solution)/shard_map/all_to_all | solution.py:169
  43.0 3.5 %reshape.95 = bf16[4,1,65536]{2,1,0:T(2,128)(2,1)} reshape(bf16[4,2,32768]{2,1,0:T(2,128)(2,1)} %all-to-all-done) | data formatting | bytes 1048576
  46.5 5.3 %reduce.1 = bf16[4,65536]{1,0:T(4,128)(2,1)} reduce(bf16[4,1,65536]{2,1,0:T(2,128)(2,1)} %reshape.95, bf16[]{:T(256)} %constant.78), dimensions={1}, to_apply=%all_to_all.7.reduce_sub_computation | reduce | bytes 1048578 | tf_op jit(solution)/shard_map/all_to_all | solution.py:169
  51.8 2.3 reshape.79
  54.0 1.3 convolution_convert_fusion
  55.3 0.0 copy-start.5
  55.3 0.0 copy-start.4
  55.4 0.0 copy-start.2
  55.4 0.9 reshape.80
  56.3 0.0 all-gather.5.cloned.1.call-update
  56.3 0.0 all-gather.3.cloned.1.call-start
  56.4 1.9 pad_maximum_fusion
  58.3 0.2 constant_dynamic-slice_fusion.2
  58.5 0.8 reshape.76
  59.3 0.0 all-gather.3.cloned.1.call-update
  59.4 0.6 dynamic-slice.1
  60.6 0.1 convert_reduce_fusion
  60.8 1.0 fusion.39
  61.8 10.3 %all-reduce = f32[2048]{0:T(1024)S(1)} all-reduce(f32[2048]{0:T(1024)S(1)} %bitcast.22), channel_id=2, replica_groups=mesh['section'=4,'dp'=4,'mp'=2] {'dp'}, use_global_device_ids=true, to_apply=%region_7.8.clone | all-reduce | flops 2048 | bytes 16384
  72.1 0.1 dynamic-slice.2
  72.2 0.6 fusion.27
  72.8 60.2 %all-gather.5.cloned.1.call-done = bf16[2048,2048]{1,0:T(8,128)(2,1)} async-done(((bf16[64,2048]{1,0:T(8,128)(2,1)}), bf16[2048,2048]{1,0:T(8,128)(2,1)}) %all-gather.5.cloned.1.call-update) | async-done | bytes 8388624 | tf_op jit(solution)/shard_map/all_gather | solution.py:179
  132.9 14.0 %convolution_convert_fusion.1 = bf16[2048,1024]{0,1:T(8,128)(2,1)} fusion(bf16[2048,2048]{1,0:T(8,128)(2,1)} %all-gather.5.cloned.1.call-done, bf16[2048,1024]{1,0:T(8,128)(2,1)} %param.15), kind=kOutput, calls=%fused_computation.20 | convolution fusion | flops 8592031744 | bytes 16777216 | tf_op jit(solution)/shard_map/dot_general | solution.py:199
  146.9 77.3 %all-gather.3.cloned.1.call-done = bf16[2048,2688]{1,0:T(8,128)(2,1)} async-done(((bf16[64,2688]{1,0:T(8,128)(2,1)}), bf16[2048,2688]{1,0:T(8,128)(2,1)}) %all-gather.3.cloned.1.call-update) | async-done | bytes 11010064 | tf_op jit(solution)/shard_map/all_gather | solution.py:166
  224.3 10.5 %fusion.9 = f32[2048,1024]{0,1:T(8,128)} fusion(bf16[1152,1024]{1,0:T(8,128)(2,1)} %param.12, bf16[2048,2688]{1,0:T(8,128)(2,1)} %all-gather.3.cloned.1.call-done), kind=kOutput, calls=%fused_computation.16 | convolution fusion | flops 4831838208 | bytes 15466496 | tf_op jit(solution)/shard_map/dot_general | solution.py:195
  234.7 13.7 %fusion.2 = (f32[2048]{0:T(1024)S(1)}, f32[2048]{0:T(1024)S(1)}, bf16[2048,1024]{0,1:T(8,128)(2,1)}) fusion(bf16[2048,1024]{0,1:T(8,128)(2,1)S(1)} %copy-done.7, f32[2048,1024]{0,1:T(8,128)} %fusion.9, bf16[1536,1024]{1,0:T(8,128)(2,1)S(1)} %copy-done, bf16[2048,2688]{1,0:T(8,128)(2,1)} %all-gather.3.cloned.1.call-done), kind=kOutput, calls=%fused_computation.8 | convolution fusion | flops 6459224064 | bytes 26230784 | tf_op jit(solution)/shard_map/dot_general | solution.py:196
  248.4 25.0 %all-reduce.1 = (f32[2048]{0:T(1024)S(1)}, f32[2048]{0:T(1024)S(1)}, f32[]{:T(128)}) all-reduce(f32[2048]{0:T(1024)S(1)} %get-tuple-element.4, f32[2048]{0:T(1024)S(1)} %get-tuple-element.3, f32[]{:T(128)} %fusion.27), channel_id=1, replica_groups=mesh['section'=4,'dp'=4,'mp'=2] {'section','mp'}, use_global_device_ids=true, to_apply=%region_5.6 | all-reduce | flops 4097 | bytes 32776 | tf_op jit(solution)/shard_map/psum | solution.py:205
  274.1 7.9 %fusion.17 = f32[384,1024]{1,0:T(8,128)} fusion(bf16[2048,2688]{1,0:T(8,128)(2,1)} %all-gather.3.cloned.1.call-done, s32[]{:T(128)S(6)} %select_n.29, bf16[2048,1024]{0,1:T(8,128)(2,1)} %convolution_convert_fusion.1, bf16[2048,1024]{0,1:T(8,128)(2,1)} %get-tuple-element.10, f32[2048]{0:T(1024)S(1)} %get-tuple-element.5, f32[2048]{0:T(1024)S(1)} %get-tuple-element.9, ...), kind=kOutput, calls=%fused_computation.24 | convolution fusion | flops 1627389952 | bytes 11558916 | tf_op jit(solution)/shard_map/dot_general | solution.py:217
  282.0 0.0 copy-done.6
  282.0 5.8 %fusion.19 = f32[288,1024]{1,0:T(8,128)} fusion(bf16[2048,2688]{1,0:T(8,128)(2,1)} %all-gather.3.cloned.1.call-done, s32[]{:T(128)S(6)} %select_n.27, bf16[2048,1024]{0,1:T(8,128)(2,1)S(1)} %copy-done.8, bf16[2048,1024]{0,1:T(8,128)(2,1)S(1)} %copy-done.6, f32[2048]{0:T(1024)S(1)} %get-tuple-element.5, f32[2048]{0:T(1024)S(1)} %get-tuple-element.9, ...), kind=kOutput, calls=%fused_computation.26 | convolution fusion | flops 1224736768 | bytes 11165700 | tf_op jit(solution)/shard_map/dot_general | solution.py:217
  287.8 5.4 %multiply_add_fusion = f32[512,1024]{1,0:T(8,128)} fusion(bf16[2048,1024]{0,1:T(8,128)(2,1)S(1)} %copy-done.6, f32[2048]{0:T(1024)S(1)} %get-tuple-element.8, bf16[2048,2048]{1,0:T(8,128)(2,1)} %all-gather.5.cloned.1.call-done, s32[]{:T(128)S(6)} %select_n.30, f32[1024]{0:T(1024)S(1)} %fusion.30, f32[512]{0:T(512)S(1)} %dynamic-slice.2), kind=kOutput, calls=%fused_computation.22 | convolution fusion | flops 2154823680 | bytes 8402948 | tf_op jit(solution)/shard_map/dot_general | solution.py:217
  (16 shorter events, 0.1 us)
Async XLA Ops:
  7.2 227.6 %copy-start = (bf16[1536,1024]{1,0:T(8,128)(2,1)S(1)}, bf16[1536,1024]{1,0:T(8,128)(2,1)}, u32[]{:S(2)}) copy-start(bf16[1536,1024]{1,0:T(8,128)(2,1)} %param.13) | copy-start | bytes 9437188
  7.2 21.8 %copy-start.3 = (s32[64,1]{0,1:T(1,128)S(1)}, s32[64,1]{0,1:T(1,128)}, u32[]{:S(2)}) copy-start(s32[64,1]{0,1:T(1,128)} %param.16) | copy-start | bytes 772
  22.1 20.9 %all-to-all-start = ((bf16[4,2,32768]{2,1,0:T(2,128)(2,1)}), bf16[4,2,32768]{2,1,0:T(2,128)(2,1)}, u32[]{:S(2)}, u32[]{:S(2)}) async-start(bf16[4,2,32768]{2,1,0:T(2,128)(2,1)} %reshape.94), calls=%async_computation | async-start | bytes 1048576 | tf_op jit(solution)/shard_map/all_to_all | solution.py:169
  28.4 104.5 %all-gather.5.cloned.1.call-start = ((), (), s32[]{:S(2)}) async-start(), calls=%async_computation.2 | async-start | bytes 8650752 | tf_op jit(solution)/shard_map/all_gather | solution.py:179
  55.3 4.0 %copy-start.5 = (u32[32]{0:T(128)S(1)}, u32[32]{0:T(128)}, u32[]{:S(2)}) copy-start(u32[32]{0:T(128)} %constant.75) | copy-start | bytes 388
  55.3 5.3 %copy-start.4 = (s32[64]{0:T(128)S(1)}, s32[64]{0:T(128)}, u32[]{:S(2)}) copy-start(s32[64]{0:T(128)} %param.17) | copy-start | bytes 772
  55.4 16.8 %copy-start.2 = (bf16[1024]{0:T(1024)(128)(2,1)S(1)}, bf16[1024]{0:T(1024)(128)(2,1)}, u32[]{:S(2)}) copy-start(bf16[1024]{0:T(1024)(128)(2,1)} %param.14) | copy-start | bytes 6148
  56.3 167.9 %all-gather.3.cloned.1.call-start = ((), (), s32[]{:S(2)}) async-start(), calls=%async_computation.1 | async-start | bytes 11354112 | tf_op jit(solution)/shard_map/all_gather | solution.py:166
  224.3 10.5 %copy-start.7 = (bf16[2048,1024]{0,1:T(8,128)(2,1)S(1)}, bf16[2048,1024]{0,1:T(8,128)(2,1)}, u32[]{:S(2)}) copy-start(bf16[2048,1024]{0,1:T(8,128)(2,1)} %convolution_convert_fusion.1) | copy-start | bytes 12582916
  274.1 7.9 %copy-start.6 = (bf16[2048,1024]{0,1:T(8,128)(2,1)S(1)}, bf16[2048,1024]{0,1:T(8,128)(2,1)}, u32[]{:S(2)}) copy-start(bf16[2048,1024]{0,1:T(8,128)(2,1)} %get-tuple-element.10) | copy-start | bytes 12582916
  274.1 7.9 %copy-start.8 = (bf16[2048,1024]{0,1:T(8,128)(2,1)S(1)}, bf16[2048,1024]{0,1:T(8,128)(2,1)}, u32[]{:S(2)}) copy-start(bf16[2048,1024]{0,1:T(8,128)(2,1)} %convolution_convert_fusion.1) | copy-start | bytes 12582916
  282.0 11.2 %copy-start.1 = (bf16[1536,1024]{1,0:T(8,128)(2,1)S(1)}, bf16[1536,1024]{1,0:T(8,128)(2,1)}, u32[]{:S(2)}) copy-start(bf16[1536,1024]{1,0:T(8,128)(2,1)} %param.13) | copy-start | bytes 9437188
Sparse Core Ops, SparseCore 0:
  56.4 76.4 all-gather.4
  136.4 87.7 all-gather.2

commit v2 on v1

--- a/solution.py
+++ b/solution.py
@@ -1,6 +1,10 @@
+import functools
+
 import jax
 import jax.numpy as jnp
 from jax import lax
+from jax.experimental import pallas as pl
+from jax.experimental.pallas import tpu as pltpu
 from jax.sharding import PartitionSpec as P
 
 D = 8192
@@ -131,6 +135,279 @@
     return (siglip_result, convnext_result, kv_result)
 
 
+FROM_X, FROM_Y, FROM_CORE, HALF_X, HALF_Y, CORE_X, CORE_Y, CORE_HX, CORE_HY = range(9)
+MESH = pl.DeviceIdType.MESH
+
+
+def gather_kernel(
+    groups,
+    sig_ref,
+    conv_ref,
+    sig_w,
+    conv_w,
+    kv_w,
+    kv_grad,
+    select,
+    f_out,
+    g_out,
+    proj,
+    ngrad,
+    f,
+    g,
+    slots,
+    mine,
+    local_sem,
+    slot_send,
+    slot_recv,
+    line_send,
+    line_recv,
+    send,
+    recv,
+    out_sem,
+):
+    section = lax.axis_index("section")
+    z = lax.axis_index("dp")
+    y = lax.axis_index("mp")
+    rows, sig = sig_ref.shape
+    conv = conv_ref.shape[1]
+    kv = kv_grad.shape[1]
+    part = rows // 8
+    wide = kv // 8
+    slot_rows = kv_grad.shape[0] // groups
+    x_section = lax.rem(section + 2, 4)
+    core_section = section + 1 - 2 * lax.rem(section, 2)
+    at_x = (x_section, z, y)
+    at_y = (section, z, 1 - y)
+    at_core = (core_section, z, y)
+
+    def number(sec, yy):
+        return sec * 2 + yy
+
+    me = number(section, y)
+    from_x, from_y = number(x_section, y), number(section, 1 - y)
+    diag = number(x_section, 1 - y)
+    core = [
+        number(core_section, y),
+        number(lax.rem(core_section + 2, 4), y),
+        number(core_section, 1 - y),
+        number(lax.rem(core_section + 2, 4), 1 - y),
+    ]
+
+    def peer(k):
+        return (section, lax.rem(z + k, groups), y)
+
+    barrier = pltpu.get_barrier_semaphore()
+    for device in [peer(k) for k in range(1, groups)] + [at_x, at_y, at_core]:
+        pl.semaphore_signal(barrier, inc=1, device_id=device, device_id_type=MESH)
+    pl.semaphore_wait(barrier, groups + 2)
+
+    def shard(is_f, q, m, half=None):
+        if is_f:
+            first, count = q * rows + m * part, part
+        else:
+            first, count = q * rows, rows
+        if half is not None:
+            count //= 2
+            first = first + half * count
+        first = pl.multiple_of(first, 32)
+        if is_f:
+            return f.at[pl.ds(first, count), :]
+        return g.at[pl.ds(first, count), pl.ds(pl.multiple_of(m * wide, 128), wide)]
+
+    def remote(ref, device, ss, rs, dst=None):
+        return pltpu.make_async_remote_copy(
+            src_ref=ref,
+            dst_ref=ref if dst is None else dst,
+            send_sem=ss,
+            recv_sem=rs,
+            device_id=device,
+            device_id_type=MESH,
+        )
+
+    sent = []
+    own = pl.ds(pl.multiple_of(z * rows, rows), rows)
+    my_cols = pl.ds(pl.multiple_of(me * wide, 128), wide)
+
+    def slot_block(q):
+        return pl.ds(pl.multiple_of(q * slot_rows, slot_rows), slot_rows)
+
+    locals_ = [
+        pltpu.make_async_copy(sig_ref, f.at[own, pl.ds(0, sig)], local_sem.at[0]),
+        pltpu.make_async_copy(conv_ref, f.at[own, pl.ds(sig, conv)], local_sem.at[1]),
+        pltpu.make_async_copy(
+            kv_grad.at[slot_block(z), my_cols], slots.at[slot_block(z), :], local_sem.at[2]
+        ),
+    ]
+    for copy in locals_:
+        copy.start()
+    for k in range(1, groups):
+        copy = remote(
+            kv_grad.at[slot_block(lax.rem(z + k, groups)), my_cols],
+            peer(k),
+            slot_send.at[k],
+            slot_recv.at[k],
+            slots.at[slot_block(z), :],
+        )
+        copy.start()
+        sent.append(copy)
+    for copy in locals_:
+        copy.wait()
+
+    def line(is_f):
+        for k in range(1, groups):
+            at = (0 if is_f else groups) + k
+            copy = remote(shard(is_f, z, me), peer(k), line_send.at[at], line_recv.at[at])
+            copy.start()
+            sent.append(copy)
+
+    line(True)
+    step = 256
+
+    def compute(is_f, q):
+        block = pl.ds(pl.multiple_of(q * rows, rows), rows)
+
+        @pl.loop(0, proj.shape[1] // step)
+        def _(n):
+            cols = pl.ds(pl.multiple_of(n * step, step), step)
+            if is_f:
+                total = jnp.dot(
+                    f[block, :sig], sig_w[:, cols], preferred_element_type=jnp.float32
+                ) + jnp.dot(f[block, sig:], conv_w[:, cols], preferred_element_type=jnp.float32)
+                proj[block, cols] = total.astype(jnp.bfloat16)
+            else:
+                total = jnp.dot(g[block, :], kv_w[:, cols], preferred_element_type=jnp.float32)
+                ngrad[block, cols] = total.astype(jnp.bfloat16)
+
+    written = []
+
+    def put(is_f, k):
+        q = lax.rem(z - k + groups, groups)
+        block = pl.ds(pl.multiple_of(q * rows, rows), rows)
+        if is_f:
+            copy = pltpu.make_async_copy(f.at[block, :], f_out.at[block, :], out_sem.at[k])
+        else:
+            copy = pltpu.make_async_copy(g.at[block, :], g_out.at[block, :], out_sem.at[groups + k])
+        copy.start()
+        written.append(copy)
+
+    put(True, 0)
+    compute(True, z)
+
+    for k in range(1, groups):
+        q = lax.rem(z - k + groups, groups)
+        ref = slots.at[slot_block(q), :]
+        remote(ref, peer(k), slot_send.at[k], slot_recv.at[k]).wait_recv()
+    mine[...] = jnp.dot(select[...], slots[...], preferred_element_type=jnp.float32).astype(
+        jnp.bfloat16
+    )
+    copy = pltpu.make_async_copy(mine, shard(False, z, me), local_sem.at[3])
+    copy.start()
+    copy.wait()
+    line(False)
+
+    items = [(False, 0), (True, 1), (True, 3), (True, 2), (False, 1), (False, 3), (False, 2)]
+
+    def go(i, ref, device, kind):
+        copy = remote(ref, device, send.at[i, kind], recv.at[i, kind])
+        copy.start()
+        sent.append(copy)
+
+    def take(i, ref, kind):
+        remote(ref, at_core, send.at[i, kind], recv.at[i, kind]).wait_recv()
+
+    def owner(i):
+        is_f, k = items[i]
+        return is_f, lax.rem(z - k + groups, groups)
+
+    def spread(i):
+        is_f, q = owner(i)
+        k = items[i][1]
+        ref = shard(is_f, q, me)
+        if k:
+            at = (0 if is_f else groups) + k
+            remote(ref, at_core, line_send.at[at], line_recv.at[at]).wait_recv()
+        go(i, ref, at_x, FROM_X)
+        go(i, ref, at_y, FROM_Y)
+        go(i, ref, at_core, FROM_CORE)
+
+    def forward(i):
+        is_f, q = owner(i)
+        take(i, shard(is_f, q, from_x), FROM_X)
+        go(i, shard(is_f, q, from_x, 0), at_y, HALF_Y)
+        go(i, shard(is_f, q, from_x), at_core, CORE_X)
+        take(i, shard(is_f, q, from_y), FROM_Y)
+        go(i, shard(is_f, q, from_y, 1), at_x, HALF_X)
+        go(i, shard(is_f, q, from_y), at_core, CORE_Y)
+
+    def halves(i):
+        is_f, q = owner(i)
+        take(i, shard(is_f, q, diag, 0), HALF_Y)
+        go(i, shard(is_f, q, diag, 0), at_core, CORE_HY)
+        take(i, shard(is_f, q, diag, 1), HALF_X)
+        go(i, shard(is_f, q, diag, 1), at_core, CORE_HX)
+
+    def finish(i):
+        is_f, q = owner(i)
+        take(i, shard(is_f, q, core[0]), FROM_CORE)
+        take(i, shard(is_f, q, core[1]), CORE_X)
+        take(i, shard(is_f, q, core[2]), CORE_Y)
+        take(i, shard(is_f, q, core[3], 0), CORE_HY)
+        take(i, shard(is_f, q, core[3], 1), CORE_HX)
+        put(is_f, items[i][1])
+        compute(is_f, q)
+
+    count = len(items)
+    for t in range(count + 3):
+        for lag, stage in enumerate((spread, forward, halves, finish)):
+            if 0 <= t - lag < count:
+                stage(t - lag)
+    for copy in sent:
+        copy.wait_send()
+    for copy in written:
+        copy.wait()
+
+
+def gather_and_project(sig_x, conv_x, sig_w, conv_w, kv_w, kv_grad, select):
+    groups = lax.axis_size("dp")
+    rows, sig = sig_x.shape
+    conv = conv_x.shape[1]
+    kv = kv_grad.shape[1]
+    share = sig_w.shape[1]
+    everything = groups * rows
+    half = jnp.bfloat16
+    hbm = pl.BlockSpec(memory_space=pl.ANY)
+    vmem = pl.BlockSpec(memory_space=pltpu.VMEM)
+    dma = pltpu.SemaphoreType.DMA
+    return pl.pallas_call(
+        functools.partial(gather_kernel, groups),
+        out_shape=(
+            jax.ShapeDtypeStruct((everything, sig + conv), half),
+            jax.ShapeDtypeStruct((everything, kv), half),
+            jax.ShapeDtypeStruct((everything, share), half),
+            jax.ShapeDtypeStruct((everything, share), half),
+        ),
+        in_specs=[hbm, hbm, vmem, vmem, vmem, hbm, vmem],
+        out_specs=(hbm, hbm, vmem, vmem),
+        scratch_shapes=[
+            pltpu.VMEM((everything, sig + conv), half),
+            pltpu.VMEM((everything, kv), half),
+            pltpu.VMEM((kv_grad.shape[0], kv // 8), half),
+            pltpu.VMEM((rows, kv // 8), half),
+            dma((4,)),
+            dma((groups,)),
+            dma((groups,)),
+            dma((2 * groups,)),
+            dma((2 * groups,)),
+            dma((2 * groups, 9)),
+            dma((2 * groups, 9)),
+            dma((2 * groups,)),
+        ],
+        compiler_params=pltpu.CompilerParams(
+            collective_id=0, has_side_effects=True, vmem_limit_bytes=56 * 2**20
+        ),
+    )(sig_x, conv_x, sig_w, conv_w, kv_w, kv_grad, select)
+
+
 def local_gathering(
     siglip_features,
     convnext_features,
@@ -144,39 +421,33 @@
     newline_grad,
 ):
     groups = lax.axis_size("dp")
-    mates = lax.axis_size("section") * lax.axis_size("mp")
     my_rank = lax.axis_index("dp")
-    me = lax.axis_index("section") * lax.axis_size("mp") + lax.axis_index("mp")
     dest_rank, source, slot_place = tile_places(tile_rank, groups)
     per_device = dest_rank.shape[0] // groups
     capacity = 2 * per_device // groups
     row_count, sig = siglip_features.shape
     conv = convnext_features.shape[1]
     tile_rows = row_count // per_device
-    part = tile_rows // mates
     kv = key_value_grad.shape[1]
-    everyone = ("dp", "section", "mp")
-
-    def my_rows(x, tiles):
-        x = x.reshape(tiles, tile_rows, x.shape[1])
-        return lax.dynamic_slice_in_dim(x, me * part, part, axis=1)
-
-    features = jnp.concatenate([siglip_features, convnext_features], axis=1)
-    features = my_rows(features, per_device).reshape(per_device * part, sig + conv)
-    features = lax.all_gather(features, everyone, axis=0, tiled=True)
-
-    slots = my_rows(key_value_grad, groups * capacity).reshape(groups, capacity * part * kv)
-    slots = lax.all_to_all(slots, "dp", split_axis=0, concat_axis=0, tiled=True)
+
     mine_dest = lax.dynamic_slice_in_dim(dest_rank, my_rank * per_device, per_device)
     mine_place = lax.dynamic_slice_in_dim(slot_place, my_rank * per_device, per_device)
-    wanted = mine_dest * capacity + mine_place
-    select = (wanted[:, None] == jnp.arange(groups * capacity, dtype=jnp.int32)[None, :]).astype(
-        jnp.bfloat16
-    )
-    grads = jnp.dot(
-        select, slots.reshape(groups * capacity, part * kv), preferred_element_type=jnp.float32
+    wanted = (mine_dest * capacity + mine_place)[:, None] * tile_rows + jnp.arange(
+        tile_rows, dtype=jnp.int32
+    )
+    select = (
+        wanted.reshape(row_count, 1)
+        == jnp.arange(groups * capacity * tile_rows, dtype=jnp.int32)[None, :]
     ).astype(jnp.bfloat16)
-    grads = lax.all_gather(grads.reshape(per_device * part, kv), everyone, axis=0, tiled=True)
+    features, grads, projected, normed_grad = gather_and_project(
+        siglip_features,
+        convnext_features,
+        siglip_projection,
+        convnext_projection,
+        key_value_weight,
+        key_value_grad,
+        select,
+    )
 
     slot_global = source * capacity + slot_place
     line_live = (dest_rank == my_rank) & (row_end == 1)
@@ -191,14 +462,7 @@
     line_vector = newline_embed.astype(jnp.float32)
     line_square = jnp.sum(line_vector * line_vector)
 
-    projected = (
-        jnp.dot(features[:, :sig], siglip_projection, preferred_element_type=jnp.float32)
-        + jnp.dot(features[:, sig:], convnext_projection, preferred_element_type=jnp.float32)
-    ).astype(jnp.bfloat16)
     proj_values = projected.astype(jnp.float32)
-    normed_grad = jnp.dot(grads, key_value_weight, preferred_element_type=jnp.float32).astype(
-        jnp.bfloat16
-    )
     grad_values = normed_grad.astype(jnp.float32)
     squares = jnp.sum(proj_values * proj_values, axis=1)
     products = jnp.sum(grad_values * proj_values, axis=1)
@@ -229,7 +493,8 @@
 def local(*args):
     rows = lax.axis_size("dp") * args[0].shape[0]
     width = args[0].shape[1] + args[1].shape[1] + args[8].shape[1]
-    if 2 * rows * width <= GATHER_LIMIT:
+    plane = (lax.axis_size("section"), lax.axis_size("dp"), lax.axis_size("mp"))
+    if 2 * rows * width <= GATHER_LIMIT and plane == (4, 4, 2):
         return local_gathering(*args)
     return local_reducing(*args)
 

time: 301 us -> 198 us (0.66)
  waiting for transfers between devices: 150 us -> 0 us
  Pallas kernels: 0 us -> 109 us
  matrix products: 59.6 us -> 18.4 us
  blocking collectives: 35.3 us -> 53.8 us
  local copies, waits for them, and re-layouts: 18 us -> 1.47 us
  between operations: 15.5 us -> 2.12 us
  starting transfers between devices: 6.36 us -> 0 us
    all_gather x2 -> x0, waiting for transfers between devices: 138 us -> none  [the longest x1 77.3 us: local_gathering(): features = lax.all_gather(features, everyone, axis=0, tiled=True)]
    pallas_call x0 -> x1, Pallas kernels: none -> 109 us  [gather_and_project(): pl.pallas_call(functools.partial(gather_kernel, groups), out_shape=(jax.S...]
    dot_general x4 -> x0, matrix products: 39.4 us -> none  [the longest x1 14 us: local_gathering(): jnp.dot(grads, key_value_weight, preferred_element_type=jnp.float32)]
    unnamed x1, blocking collectives: 10.3 us -> 27.6 us
    all_to_all x1 -> x0, waiting for transfers between devices: 12.8 us -> none  [local_gathering(): slots = lax.all_to_all(slots, 'dp', split_axis=0, concat_axis=0, tiled=True)]
    all_to_all x2 -> x0, other arithmetic: 11.2 us -> none  [local_gathering(): slots = lax.all_to_all(slots, 'dp', split_axis=0, concat_axis=0, tiled=True)]
    all_to_all x1 -> x0, starting transfers between devices: 6.32 us -> none  [local_gathering(): slots = lax.all_to_all(slots, 'dp', split_axis=0, concat_axis=0, tiled=True)]
    unnamed x23 -> x17, local copies, waits for them, and re-layouts: 7.07 us -> 1.22 us
  transfers between devices with their start and end apart: 3 -> 0, of which waited for: 3 -> 0; matrix products, arithmetic and copies ran while one was open for 7% -> 0% of each run, Pallas kernels for 0% -> 0%
where the time goes in v2:
time: 198 us
  Pallas kernels  109 us (55%)
  blocking collectives  53.8 us (27%)
  matrix products  18.4 us (9%)
  other arithmetic  13.4 us (7%)
  between operations  2.12 us (1%)
    pallas_call x1, Pallas kernels, gather_and_project(): pl.pallas_call(functools.partial(gather_kernel, groups), out_shape=(jax.S...  109 us
    unnamed x1, blocking collectives  27.6 us
    psum x1, blocking collectives, local_gathering(): lax.psum((squares, products, line_square), ('section', 'mp'))  26.1 us
    dot_general x3, matrix products, contract(): lax.dot_general(a, b, (((0,), (0,)), ((), ())), preferred_element_type=jn...  18.3 us
    reduce_sum x1, other arithmetic, local_gathering(): squares = jnp.sum(proj_values * proj_values, axis=1)  5.21 us

profile of v2, /device:TPU:0, one launch (start us, length us, event | category | flops | bytes accessed | tf_op | source)
XLA Modules:
  0.0 197.7 jit_solution(14902576372896346378)
XLA Ops:
  0.6 0.0 copy-start
  0.6 0.5 broadcast.78
  1.2 1.3 reduce.3
  2.5 0.1 eq.55
  2.6 0.1 fusion.20
  2.7 0.2 select_reduce_fusion
  2.9 0.1 reshape.71
  3.0 0.7 fusion.36
  3.7 0.1 iota_add_fusion
  3.8 0.1 add.75
  3.9 1.2 fusion.11.select
  5.1 108.5 %shard_map.121 = (bf16[2048,2688]{1,0:T(8,128)(2,1)}, bf16[2048,2048]{1,0:T(8,128)(2,1)}, bf16[2048,1024]{1,0:T(8,128)(2,1)}, bf16[2048,1024]{1,0:T(8,128)(2,1)}) custom-call(bf16[512,1152]{1,0:T(8,128)(2,1)} %sig_ref.1, bf16[512,1536]{1,0:T(8,128)(2,1)} %conv_ref.1, bf16[1152,1024]{1,0:T(8,128)(2,1)} %sig_w.1, bf16[1536,1024]{1,0:T(8,128)(2,1)} %conv_w.1, ...), custom_call_target="tpu_custom_call" | custom-call | tf_op jit(solution)/shard_map/pallas_call | solution.py:381
  113.6 0.0 copy-start.3
  113.7 0.0 copy-start.4
  113.7 0.0 copy-start.5
  113.7 0.0 copy-start.6
  113.7 5.2 %fusion.2 = (f32[2048]{0:T(1024)S(1)}, f32[2048]{0:T(1024)S(1)}) fusion(bf16[2048,1024]{1,0:T(8,128)(2,1)} %get-tuple-element.8, bf16[2048,1024]{1,0:T(8,128)(2,1)} %get-tuple-element.9), kind=kLoop, calls=%fused_computation.7 | loop fusion | flops 12578816 | bytes 8404992 | tf_op jit(solution)/shard_map/reduce_sum | solution.py:467
  118.9 0.0 copy-done.3
  118.9 0.6 fusion.22
  119.5 26.1 %all-reduce.1 = (f32[2048]{0:T(1024)S(1)}, f32[2048]{0:T(1024)S(1)}, f32[]{:T(128)}) all-reduce(f32[2048]{0:T(1024)S(1)} %get-tuple-element.12, f32[2048]{0:T(1024)S(1)} %get-tuple-element.11, f32[]{:T(128)} %fusion.22), channel_id=1, replica_groups=mesh['section'=4,'dp'=4,'mp'=2] {'section','mp'}, use_global_device_ids=true, to_apply=%region_5.6 | all-reduce | flops 4097 | bytes 32776 | tf_op jit(solution)/shard_map/psum | solution.py:469
  146.4 0.0 copy-done.4
  146.4 0.0 copy-done.5
  146.4 0.1 convert_reduce_fusion
  146.5 0.0 copy-done
  146.5 0.1 fusion.33
  146.7 27.6 %all-reduce = f32[2048]{0:T(1024)S(1)} all-reduce(f32[2048]{0:T(1024)S(1)} %bitcast.17), channel_id=2, replica_groups=mesh['section'=4,'dp'=4,'mp'=2] {'dp'}, use_global_device_ids=true, to_apply=%region_7.8.clone | all-reduce | flops 2048 | bytes 16384
  174.3 0.0 copy-done.6
  174.3 0.6 dynamic-slice.1
  175.6 0.1 dynamic-slice.2
  175.7 0.0 copy-start.1
  175.7 0.0 copy-start.2
  175.7 6.8 %multiply_add_fusion = f32[512,1024]{1,0:T(8,128)} fusion(bf16[2048,1024]{1,0:T(8,128)(2,1)} %get-tuple-element.8, f32[2048]{0:T(1024)S(1)} %get-tuple-element.16, bf16[2048,2048]{1,0:T(8,128)(2,1)} %get-tuple-element.10, s32[]{:T(128)S(6)} %select_n.25, f32[1024]{0:T(1024)S(1)} %fusion.24, f32[512]{0:T(512)S(1)} %dynamic-slice.2), kind=kOutput, calls=%fused_computation.14 | convolution fusion | flops 2154823680 | bytes 8402948 | tf_op jit(solution)/shard_map/dot_general | solution.py:481
  182.4 0.0 copy-done.1
  182.4 0.0 copy-done.2
  182.4 3.7 %fusion.1 = bf16[2048,1024]{1,0:T(8,128)(2,1)} fusion(bf16[2048,1024]{1,0:T(8,128)(2,1)S(1)} %copy-done.2, bf16[2048,1024]{1,0:T(8,128)(2,1)S(1)} %copy-done.1, f32[2048]{0:T(1024)S(1)} %get-tuple-element.13, f32[2048]{0:T(1024)S(1)} %get-tuple-element.17, f32[2048]{0:T(1024)S(1)} %get-tuple-element.16), kind=kLoop, calls=%fused_computation.6 | loop fusion | flops 16777216 | bytes 12607488 | tf_op jit(solution)/shard_map/convert_element_type | solution.py:475
  186.2 5.6 %fusion.12 = f32[384,1024]{1,0:T(8,128)} fusion(bf16[2048,1024]{1,0:T(8,128)(2,1)} %fusion.1, bf16[2048,2688]{1,0:T(8,128)(2,1)} %get-tuple-element.7, s32[]{:T(128)S(6)} %select_n.24), kind=kOutput, calls=%fused_computation.18 | convolution fusion | flops 1610612736 | bytes 7340036 | tf_op jit(solution)/shard_map/dot_general | solution.py:481
  191.8 5.9 %fusion.14 = f32[288,1024]{1,0:T(8,128)} fusion(bf16[2048,1024]{1,0:T(8,128)(2,1)} %fusion.1, bf16[2048,2688]{1,0:T(8,128)(2,1)} %get-tuple-element.7, s32[]{:T(128)S(6)} %select_n.23), kind=kOutput, calls=%fused_computation.20 | convolution fusion | flops 1207959552 | bytes 6946820 | tf_op jit(solution)/shard_map/dot_general | solution.py:481
  (5 shorter events, 0.1 us)
Async XLA Ops:
  0.6 145.9 %copy-start = (bf16[32,2048]{1,0:T(8,128)(2,1)S(1)}, bf16[32,2048]{1,0:T(8,128)(2,1)}, u32[]{:S(2)}) copy-start(bf16[32,2048]{1,0:T(8,128)(2,1)} %param.19) | copy-start | bytes 393220
  113.6 5.3 %copy-start.3 = (bf16[1024]{0:T(1024)(128)(2,1)S(1)}, bf16[1024]{0:T(1024)(128)(2,1)}, u32[]{:S(2)}) copy-start(bf16[1024]{0:T(1024)(128)(2,1)} %param.14) | copy-start | bytes 6148
  113.7 32.7 %copy-start.4 = (s32[64,1]{0,1:T(1,128)S(1)}, s32[64,1]{0,1:T(1,128)}, u32[]{:S(2)}) copy-start(s32[64,1]{0,1:T(1,128)} %param.16) | copy-start | bytes 772
  113.7 32.7 %copy-start.5 = (s32[64]{0:T(128)S(1)}, s32[64]{0:T(128)}, u32[]{:S(2)}) copy-start(s32[64]{0:T(128)} %param.17) | copy-start | bytes 772
  113.7 60.6 %copy-start.6 = (u32[32]{0:T(128)S(1)}, u32[32]{0:T(128)}, u32[]{:S(2)}) copy-start(u32[32]{0:T(128)} %constant.67) | copy-start | bytes 388
  175.7 6.8 %copy-start.1 = (bf16[2048,1024]{1,0:T(8,128)(2,1)S(1)}, bf16[2048,1024]{1,0:T(8,128)(2,1)}, u32[]{:S(2)}) copy-start(bf16[2048,1024]{1,0:T(8,128)(2,1)} %get-tuple-element.8) | copy-start | bytes 12582916
  175.7 6.8 %copy-start.2 = (bf16[2048,1024]{1,0:T(8,128)(2,1)S(1)}, bf16[2048,1024]{1,0:T(8,128)(2,1)}, u32[]{:S(2)}) copy-start(bf16[2048,1024]{1,0:T(8,128)(2,1)} %get-tuple-element.9) | copy-start | bytes 12582916

commit v3 on v2

--- a/solution.py
+++ b/solution.py
@@ -143,17 +143,29 @@
     groups,
     sig_ref,
     conv_ref,
+    sig_w_ref,
+    conv_w_ref,
+    kv_w_ref,
+    kv_grad,
+    select,
+    line_part,
+    line_sq,
+    f_out,
+    g_out,
+    p_out,
+    n_out,
+    stats_out,
+    line_out,
+    f,
+    g,
+    proj,
+    ngrad,
     sig_w,
     conv_w,
     kv_w,
-    kv_grad,
-    select,
-    f_out,
-    g_out,
-    proj,
-    ngrad,
-    f,
-    g,
+    acc,
+    stats,
+    line_all,
     slots,
     mine,
     local_sem,
@@ -164,6 +176,10 @@
     send,
     recv,
     out_sem,
+    stat_send,
+    stat_recv,
+    sum_send,
+    sum_recv,
 ):
     section = lax.axis_index("section")
     z = lax.axis_index("dp")
@@ -196,10 +212,20 @@
     def peer(k):
         return (section, lax.rem(z + k, groups), y)
 
+    def mate(j):
+        p = lax.rem(me + j, 8)
+        return (lax.div(p, 2), z, lax.rem(p, 2))
+
+    weights = [
+        pltpu.make_async_copy(sig_w_ref, sig_w, local_sem.at[4]),
+        pltpu.make_async_copy(conv_w_ref, conv_w, local_sem.at[5]),
+        pltpu.make_async_copy(kv_w_ref, kv_w, local_sem.at[6]),
+    ]
+
     barrier = pltpu.get_barrier_semaphore()
-    for device in [peer(k) for k in range(1, groups)] + [at_x, at_y, at_core]:
+    for device in [peer(k) for k in range(1, groups)] + [mate(j) for j in range(1, 8)]:
         pl.semaphore_signal(barrier, inc=1, device_id=device, device_id_type=MESH)
-    pl.semaphore_wait(barrier, groups + 2)
+    pl.semaphore_wait(barrier, groups + 6)
 
     def shard(is_f, q, m, half=None):
         if is_f:
@@ -250,6 +276,17 @@
         )
         copy.start()
         sent.append(copy)
+    for k in range(1, groups):
+        copy = remote(
+            line_part.at[lax.rem(z + k, groups)],
+            peer(k),
+            sum_send.at[k],
+            sum_recv.at[k],
+            line_all.at[z],
+        )
+        copy.start()
+        sent.append(copy)
+    line_all[z] = line_part[z]
     for copy in locals_:
         copy.wait()
 
@@ -261,10 +298,15 @@
             sent.append(copy)
 
     line(True)
+    for copy in weights:
+        copy.start()
     step = 256
 
     def compute(is_f, q):
         block = pl.ds(pl.multiple_of(q * rows, rows), rows)
+
+        if not is_f:
+            acc[...] = jnp.zeros_like(acc)
 
         @pl.loop(0, proj.shape[1] // step)
         def _(n):
@@ -276,7 +318,31 @@
                 proj[block, cols] = total.astype(jnp.bfloat16)
             else:
                 total = jnp.dot(g[block, :], kv_w[:, cols], preferred_element_type=jnp.float32)
-                ngrad[block, cols] = total.astype(jnp.bfloat16)
+                rounded = total.astype(jnp.bfloat16)
+                ngrad[block, cols] = rounded
+                gv = rounded.astype(jnp.float32)
+                pv = proj[block, cols].astype(jnp.float32)
+                sq, pr = pv * pv, gv * pv
+                acc[0] += sq[:, :128] + sq[:, 128:]
+                acc[1] += pr[:, :128] + pr[:, 128:]
+
+    def share_stats(k):
+        stats[me, k, 0:1, :] = jnp.sum(acc[0].T, axis=0, keepdims=True)
+        stats[me, k, 1:2, :] = jnp.sum(acc[1].T, axis=0, keepdims=True)
+        stats[me, k, 2:8, :] = line_sq[2:8, :]
+        for j in range(1, 8):
+            copy = remote(stats.at[me, k], mate(j), stat_send.at[k, j], stat_recv.at[k, j])
+            copy.start()
+            sent.append(copy)
+
+    def result(is_f, k):
+        q = lax.rem(z - k + groups, groups)
+        block = pl.ds(pl.multiple_of(q * rows, rows), rows)
+        here, there = (proj, p_out) if is_f else (ngrad, n_out)
+        at = (2 if is_f else 3) * groups + k
+        copy = pltpu.make_async_copy(here.at[block, :], there.at[block, :], out_sem.at[at])
+        copy.start()
+        written.append(copy)
 
     written = []
 
@@ -291,7 +357,10 @@
         written.append(copy)
 
     put(True, 0)
+    for copy in weights:
+        copy.wait()
     compute(True, z)
+    result(True, 0)
 
     for k in range(1, groups):
         q = lax.rem(z - k + groups, groups)
@@ -355,19 +424,36 @@
         take(i, shard(is_f, q, core[3], 1), CORE_HX)
         put(is_f, items[i][1])
         compute(is_f, q)
+        if not is_f:
+            share_stats(items[i][1])
+        result(is_f, items[i][1])
 
     count = len(items)
     for t in range(count + 3):
         for lag, stage in enumerate((spread, forward, halves, finish)):
             if 0 <= t - lag < count:
                 stage(t - lag)
+    for k in range(1, groups):
+        q = lax.rem(z - k + groups, groups)
+        remote(line_all.at[q], peer(k), sum_send.at[k], sum_recv.at[k]).wait_recv()
+    line_out[...] = sum([line_all[q] for q in range(1, groups)], line_all[0])
+    for is_f, k in items:
+        if is_f:
+            continue
+        for j in range(1, 8):
+            ref = stats.at[lax.rem(me - j + 8, 8), k]
+            remote(ref, mate(j), stat_send.at[k, j], stat_recv.at[k, j]).wait_recv()
+        q = lax.rem(z - k + groups, groups)
+        stats_out[:, pl.ds(pl.multiple_of(q * rows, rows), rows)] = sum(
+            [stats[m, k] for m in range(1, 8)], stats[0, k]
+        )
     for copy in sent:
         copy.wait_send()
     for copy in written:
         copy.wait()
 
 
-def gather_and_project(sig_x, conv_x, sig_w, conv_w, kv_w, kv_grad, select):
+def gather_and_project(sig_x, conv_x, sig_w, conv_w, kv_w, kv_grad, select, line_part, line_sq):
     groups = lax.axis_size("dp")
     rows, sig = sig_x.shape
     conv = conv_x.shape[1]
@@ -385,27 +471,41 @@
             jax.ShapeDtypeStruct((everything, kv), half),
             jax.ShapeDtypeStruct((everything, share), half),
             jax.ShapeDtypeStruct((everything, share), half),
+            jax.ShapeDtypeStruct((8, everything), jnp.float32),
+            jax.ShapeDtypeStruct((8, kv // groups), jnp.float32),
         ),
-        in_specs=[hbm, hbm, vmem, vmem, vmem, hbm, vmem],
-        out_specs=(hbm, hbm, vmem, vmem),
+        in_specs=[hbm, hbm, hbm, hbm, hbm, hbm, vmem, vmem, vmem],
+        out_specs=(hbm, hbm, hbm, hbm, vmem, vmem),
         scratch_shapes=[
             pltpu.VMEM((everything, sig + conv), half),
             pltpu.VMEM((everything, kv), half),
+            pltpu.VMEM((everything, share), half),
+            pltpu.VMEM((everything, share), half),
+            pltpu.VMEM(sig_w.shape, half),
+            pltpu.VMEM(conv_w.shape, half),
+            pltpu.VMEM(kv_w.shape, half),
+            pltpu.VMEM((2, rows, 128), jnp.float32),
+            pltpu.VMEM((8, groups, 8, rows), jnp.float32),
+            pltpu.VMEM((groups, 8, kv // groups), jnp.float32),
             pltpu.VMEM((kv_grad.shape[0], kv // 8), half),
             pltpu.VMEM((rows, kv // 8), half),
-            dma((4,)),
+            dma((7,)),
             dma((groups,)),
             dma((groups,)),
             dma((2 * groups,)),
             dma((2 * groups,)),
             dma((2 * groups, 9)),
             dma((2 * groups, 9)),
-            dma((2 * groups,)),
+            dma((4 * groups,)),
+            dma((groups, 8)),
+            dma((groups, 8)),
+            dma((groups,)),
+            dma((groups,)),
         ],
         compiler_params=pltpu.CompilerParams(
             collective_id=0, has_side_effects=True, vmem_limit_bytes=56 * 2**20
         ),
-    )(sig_x, conv_x, sig_w, conv_w, kv_w, kv_grad, select)
+    )(sig_x, conv_x, sig_w, conv_w, kv_w, kv_grad, select, line_part, line_sq)
 
 
 def local_gathering(
@@ -439,7 +539,21 @@
         wanted.reshape(row_count, 1)
         == jnp.arange(groups * capacity * tile_rows, dtype=jnp.int32)[None, :]
     ).astype(jnp.bfloat16)
-    features, grads, projected, normed_grad = gather_and_project(
+    slot_global = source * capacity + slot_place
+    line_live = (dest_rank == my_rank) & (row_end == 1)
+    slot_ids = jnp.arange(groups * capacity, dtype=jnp.int32)[None, :]
+    newline_mask = jnp.sum(
+        ((slot_global[:, None] == slot_ids) & line_live[:, None]).astype(jnp.int32), axis=0
+    )
+    line_total = jnp.dot(
+        newline_mask.astype(jnp.bfloat16)[None, :], newline_grad, preferred_element_type=jnp.float32
+    )[0]
+    line_part = jnp.broadcast_to(
+        line_total.reshape(groups, 1, kv // groups), (groups, 8, kv // groups)
+    )
+    line_vector = newline_embed.astype(jnp.float32)
+    line_square = jnp.sum(line_vector * line_vector)
+    features, grads, projected, normed_grad, stats, line_total = gather_and_project(
         siglip_features,
         convnext_features,
         siglip_projection,
@@ -447,26 +561,14 @@
         key_value_weight,
         key_value_grad,
         select,
-    )
-
-    slot_global = source * capacity + slot_place
-    line_live = (dest_rank == my_rank) & (row_end == 1)
-    slot_ids = jnp.arange(groups * capacity, dtype=jnp.int32)[None, :]
-    newline_mask = jnp.sum(
-        ((slot_global[:, None] == slot_ids) & line_live[:, None]).astype(jnp.int32), axis=0
-    )
-    line_total = jnp.dot(
-        newline_mask.astype(jnp.bfloat16)[None, :], newline_grad, preferred_element_type=jnp.float32
-    )[0]
-    line_total = lax.psum_scatter(line_total, "dp", scatter_dimension=0, tiled=True)
-    line_vector = newline_embed.astype(jnp.float32)
-    line_square = jnp.sum(line_vector * line_vector)
+        line_part,
+        jnp.full((8, row_count), line_square),
+    )
+    squares, products, line_square = stats[0], stats[1], stats[2, 0]
+    line_total = line_total[0]
 
     proj_values = projected.astype(jnp.float32)
     grad_values = normed_grad.astype(jnp.float32)
-    squares = jnp.sum(proj_values * proj_values, axis=1)
-    products = jnp.sum(grad_values * proj_values, axis=1)
-    squares, products, line_square = lax.psum((squares, products, line_square), ("section", "mp"))
     inverse = lax.rsqrt(squares / D + epsilon)[:, None]
     normed = (proj_values * inverse).astype(jnp.bfloat16)
     line_normed = (line_vector * lax.rsqrt(line_square / D + epsilon)).astype(jnp.bfloat16)

time: 198 us -> 165 us (0.83)
  the two profiles are of different devices: /device:TPU:0 before, /device:TPU:9 now
where the time goes in v3:
time: 165 us
  Pallas kernels  129 us (78%)
  matrix products  19.3 us (12%)
  other arithmetic  10.5 us (6%)
  local copies, waits for them, and re-layouts  4.62 us (3%)
    pallas_call x1, Pallas kernels, gather_and_project(): pl.pallas_call(functools.partial(gather_kernel, groups), out_shape=(jax.S...  129 us
    dot_general x3, matrix products, contract(): lax.dot_general(a, b, (((0,), (0,)), ((), ())), preferred_element_type=jn...  18.3 us
    convert_element_type x1, other arithmetic, local_gathering(): projected_grad = (inverse * grad_values - inverse ** 3 * proj_values * pr...  3.76 us

profile of v3, /device:TPU:9, one launch (start us, length us, event | category | flops | bytes accessed | tf_op | source)
XLA Modules:
  0.0 164.8 jit_solution(5264643427775050512)
XLA Ops:
  0.6 0.5 broadcast.93
  1.1 1.3 reduce.3
  2.5 0.1 eq.55
  2.6 0.1 fusion.21
  2.7 0.2 select_reduce_fusion
  2.9 0.1 reshape.98
  3.0 0.7 fusion.36
  3.7 0.1 iota_add_fusion
  3.8 0.1 add.76
  3.9 1.2 fusion.9.select
  5.1 0.7 bitcast_and_fusion
  5.8 0.1 convert_reduce_fusion
  5.9 1.0 fusion.18
  6.9 0.6 broadcast_in_dim.4.line_part
  7.6 1.4 fusion.23
  8.9 1.3 broadcast_in_dim.5.line_sq
  10.2 0.0 copy-start.2
  10.2 128.9 %shard_map.121 = (bf16[2048,2688]{1,0:T(8,128)(2,1)}, bf16[2048,2048]{1,0:T(8,128)(2,1)}, bf16[2048,1024]{1,0:T(8,128)(2,1)}, bf16[2048,1024]{1,0:T(8,128)(2,1)}, f32[8,2048]{1,0:T(8,128)}, /*index=5*/f32[8,512]{1,0:T(8,128)}) custom-call(bf16[512,1152]{1,0:T(8,128)(2,1)} %sig_ref.1, bf16[512,1536]{1,0:T(8,128)(2,1)} %conv_ref.1, ...), custom_call_target="tpu_custom_call" | custom-call | tf_op jit(solution)/shard_map/pallas_call | solution.py:467
  139.1 0.9 add_rsqrt_fusion
  140.1 1.2 slice.15
  142.0 0.0 copy-done.2
  142.0 0.7 slice.14
  142.7 0.0 copy-start
  142.7 0.0 copy-start.1
  142.7 6.8 %multiply_add_fusion = f32[512,1024]{1,0:T(8,128)} fusion(bf16[2048,1024]{1,0:T(8,128)(2,1)} %get-tuple-element.12, f32[2048]{0:T(1024)S(1)} %bitcast.27, bf16[2048,2048]{1,0:T(8,128)(2,1)} %get-tuple-element.13, s32[]{:T(128)S(6)} %select_n.26, f32[1024]{0:T(1024)S(1)} %fusion.25, f32[512]{0:T(512)S(1)} %bitcast.32), kind=kOutput, calls=%fused_computation.9 | convolution fusion | flops 2154823680 | bytes 8402948 | tf_op jit(solution)/shard_map/dot_general | solution.py:583
  149.5 0.0 copy-done
  149.5 0.0 copy-done.1
  149.5 3.8 %fusion.3 = bf16[2048,1024]{1,0:T(8,128)(2,1)} fusion(bf16[2048,1024]{1,0:T(8,128)(2,1)S(1)} %copy-done, bf16[2048,1024]{1,0:T(8,128)(2,1)S(1)} %copy-done.1, f32[2048]{0:T(1024)S(1)} %bitcast.31, f32[2048]{0:T(1024)S(1)} %multiply_multiply_fusion, f32[2048]{0:T(1024)S(1)} %bitcast.29), kind=kLoop, calls=%fused_computation.5 | loop fusion | flops 16777216 | bytes 12607488 | tf_op jit(solution)/shard_map/convert_element_type | solution.py:577
  153.2 5.6 %fusion.10 = f32[384,1024]{1,0:T(8,128)} fusion(bf16[2048,1024]{1,0:T(8,128)(2,1)} %fusion.3, bf16[2048,2688]{1,0:T(8,128)(2,1)} %get-tuple-element.9, s32[]{:T(128)S(6)} %select_n.25), kind=kOutput, calls=%fused_computation.13 | convolution fusion | flops 1610612736 | bytes 7340036 | tf_op jit(solution)/shard_map/dot_general | solution.py:583
  158.9 5.9 %fusion.12 = f32[288,1024]{1,0:T(8,128)} fusion(bf16[2048,1024]{1,0:T(8,128)(2,1)} %fusion.3, bf16[2048,2688]{1,0:T(8,128)(2,1)} %get-tuple-element.9, s32[]{:T(128)S(6)} %select_n.24), kind=kOutput, calls=%fused_computation.15 | convolution fusion | flops 1207959552 | bytes 6946820 | tf_op jit(solution)/shard_map/dot_general | solution.py:583
  (5 shorter events, 0.1 us)
Async XLA Ops:
  10.2 131.7 %copy-start.2 = (bf16[1024]{0:T(1024)(128)(2,1)S(1)}, bf16[1024]{0:T(1024)(128)(2,1)}, u32[]{:S(2)}) copy-start(bf16[1024]{0:T(1024)(128)(2,1)} %param.14) | copy-start | bytes 6148
  142.7 6.8 %copy-start = (bf16[2048,1024]{1,0:T(8,128)(2,1)S(1)}, bf16[2048,1024]{1,0:T(8,128)(2,1)}, u32[]{:S(2)}) copy-start(bf16[2048,1024]{1,0:T(8,128)(2,1)} %get-tuple-element.12) | copy-start | bytes 12582916
  142.7 6.8 %copy-start.1 = (bf16[2048,1024]{1,0:T(8,128)(2,1)S(1)}, bf16[2048,1024]{1,0:T(8,128)(2,1)}, u32[]{:S(2)}) copy-start(bf16[2048,1024]{1,0:T(8,128)(2,1)} %get-tuple-element.11) | copy-start | bytes 12582916

commit v4 on v3

--- a/solution.py
+++ b/solution.py
@@ -291,7 +291,7 @@
         copy.wait()
 
     def line(is_f):
-        for k in range(1, groups):
+        for k in (1, 3, 2):
             at = (0 if is_f else groups) + k
             copy = remote(shard(is_f, z, me), peer(k), line_send.at[at], line_recv.at[at])
             copy.start()
@@ -428,11 +428,15 @@
             share_stats(items[i][1])
         result(is_f, items[i][1])
 
-    count = len(items)
-    for t in range(count + 3):
-        for lag, stage in enumerate((spread, forward, halves, finish)):
-            if 0 <= t - lag < count:
-                stage(t - lag)
+    order = [
+        (spread, 0), (spread, 1), (forward, 0), (spread, 2), (forward, 1), (halves, 0),
+        (spread, 3), (forward, 2), (halves, 1), (finish, 0), (forward, 3), (halves, 2),
+        (spread, 4), (finish, 1), (halves, 3), (spread, 5), (finish, 2), (forward, 4),
+        (halves, 4), (spread, 6), (finish, 3), (forward, 5), (halves, 5), (forward, 6),
+        (finish, 4), (halves, 6), (finish, 5), (finish, 6),
+    ]
+    for stage, i in order:
+        stage(i)
     for k in range(1, groups):
         q = lax.rem(z - k + groups, groups)
         remote(line_all.at[q], peer(k), sum_send.at[k], sum_recv.at[k]).wait_recv()

time: 165 us -> 157 us (0.952)
  the two profiles are of different devices: /device:TPU:9 before, /device:TPU:0 now
where the time goes in v4:
time: 157 us
  Pallas kernels  121 us (77%)
  matrix products  19.3 us (12%)
  other arithmetic  10.5 us (7%)
  local copies, waits for them, and re-layouts  4.62 us (3%)
    pallas_call x1, Pallas kernels, gather_and_project(): pl.pallas_call(functools.partial(gather_kernel, groups), out_shape=(jax.S...  121 us
    dot_general x3, matrix products, contract(): lax.dot_general(a, b, (((0,), (0,)), ((), ())), preferred_element_type=jn...  18.3 us
    convert_element_type x1, other arithmetic, local_gathering(): projected_grad = (inverse * grad_values - inverse ** 3 * proj_values * pr...  3.76 us

profile of v4, /device:TPU:0, one launch (start us, length us, event | category | flops | bytes accessed | tf_op | source)
XLA Modules:
  0.0 156.6 jit_solution(10715139665647999783)
XLA Ops:
  0.6 0.5 broadcast.93
  1.1 1.3 reduce.3
  2.5 0.1 eq.55
  2.6 0.1 fusion.21
  2.7 0.2 select_reduce_fusion
  2.9 0.1 reshape.98
  3.0 0.7 fusion.36
  3.7 0.1 iota_add_fusion
  3.8 0.1 add.76
  3.9 1.2 fusion.9.select
  5.1 0.7 bitcast_and_fusion
  5.8 0.1 convert_reduce_fusion
  5.9 1.0 fusion.18
  6.9 0.6 broadcast_in_dim.4.line_part
  7.6 1.4 fusion.23
  8.9 1.3 broadcast_in_dim.5.line_sq
  10.2 0.0 copy-start.2
  10.2 120.7 %shard_map.121 = (bf16[2048,2688]{1,0:T(8,128)(2,1)}, bf16[2048,2048]{1,0:T(8,128)(2,1)}, bf16[2048,1024]{1,0:T(8,128)(2,1)}, bf16[2048,1024]{1,0:T(8,128)(2,1)}, f32[8,2048]{1,0:T(8,128)}, /*index=5*/f32[8,512]{1,0:T(8,128)}) custom-call(bf16[512,1152]{1,0:T(8,128)(2,1)} %sig_ref.1, bf16[512,1536]{1,0:T(8,128)(2,1)} %conv_ref.1, ...), custom_call_target="tpu_custom_call" | custom-call | tf_op jit(solution)/shard_map/pallas_call | solution.py:471
  131.0 0.9 add_rsqrt_fusion
  131.9 1.2 slice.15
  133.8 0.0 copy-done.2
  133.8 0.7 slice.14
  134.6 0.0 copy-start
  134.6 0.0 copy-start.1
  134.6 6.8 %multiply_add_fusion = f32[512,1024]{1,0:T(8,128)} fusion(bf16[2048,1024]{1,0:T(8,128)(2,1)} %get-tuple-element.12, f32[2048]{0:T(1024)S(1)} %bitcast.27, bf16[2048,2048]{1,0:T(8,128)(2,1)} %get-tuple-element.13, s32[]{:T(128)S(6)} %select_n.26, f32[1024]{0:T(1024)S(1)} %fusion.25, f32[512]{0:T(512)S(1)} %bitcast.32), kind=kOutput, calls=%fused_computation.9 | convolution fusion | flops 2154823680 | bytes 8402948 | tf_op jit(solution)/shard_map/dot_general | solution.py:587
  141.3 0.0 copy-done
  141.3 0.0 copy-done.1
  141.3 3.8 %fusion.3 = bf16[2048,1024]{1,0:T(8,128)(2,1)} fusion(bf16[2048,1024]{1,0:T(8,128)(2,1)S(1)} %copy-done, bf16[2048,1024]{1,0:T(8,128)(2,1)S(1)} %copy-done.1, f32[2048]{0:T(1024)S(1)} %bitcast.31, f32[2048]{0:T(1024)S(1)} %multiply_multiply_fusion, f32[2048]{0:T(1024)S(1)} %bitcast.29), kind=kLoop, calls=%fused_computation.5 | loop fusion | flops 16777216 | bytes 12607488 | tf_op jit(solution)/shard_map/convert_element_type | solution.py:581
  145.1 5.6 %fusion.10 = f32[384,1024]{1,0:T(8,128)} fusion(bf16[2048,1024]{1,0:T(8,128)(2,1)} %fusion.3, bf16[2048,2688]{1,0:T(8,128)(2,1)} %get-tuple-element.9, s32[]{:T(128)S(6)} %select_n.25), kind=kOutput, calls=%fused_computation.13 | convolution fusion | flops 1610612736 | bytes 7340036 | tf_op jit(solution)/shard_map/dot_general | solution.py:587
  150.7 5.9 %fusion.12 = f32[288,1024]{1,0:T(8,128)} fusion(bf16[2048,1024]{1,0:T(8,128)(2,1)} %fusion.3, bf16[2048,2688]{1,0:T(8,128)(2,1)} %get-tuple-element.9, s32[]{:T(128)S(6)} %select_n.24), kind=kOutput, calls=%fused_computation.15 | convolution fusion | flops 1207959552 | bytes 6946820 | tf_op jit(solution)/shard_map/dot_general | solution.py:587
  (5 shorter events, 0.1 us)
Async XLA Ops:
  10.2 123.6 %copy-start.2 = (bf16[1024]{0:T(1024)(128)(2,1)S(1)}, bf16[1024]{0:T(1024)(128)(2,1)}, u32[]{:S(2)}) copy-start(bf16[1024]{0:T(1024)(128)(2,1)} %param.14) | copy-start | bytes 6148
  134.6 6.8 %copy-start = (bf16[2048,1024]{1,0:T(8,128)(2,1)S(1)}, bf16[2048,1024]{1,0:T(8,128)(2,1)}, u32[]{:S(2)}) copy-start(bf16[2048,1024]{1,0:T(8,128)(2,1)} %get-tuple-element.12) | copy-start | bytes 12582916
  134.6 6.8 %copy-start.1 = (bf16[2048,1024]{1,0:T(8,128)(2,1)S(1)}, bf16[2048,1024]{1,0:T(8,128)(2,1)}, u32[]{:S(2)}) copy-start(bf16[2048,1024]{1,0:T(8,128)(2,1)} %get-tuple-element.11) | copy-start | bytes 12582916

commit v5 on v4

--- a/solution.py
+++ b/solution.py
@@ -150,7 +150,8 @@
     select,
     line_part,
     line_sq,
-    f_out,
+    sig_out,
+    conv_out,
     g_out,
     p_out,
     n_out,
@@ -350,11 +351,18 @@
         q = lax.rem(z - k + groups, groups)
         block = pl.ds(pl.multiple_of(q * rows, rows), rows)
         if is_f:
-            copy = pltpu.make_async_copy(f.at[block, :], f_out.at[block, :], out_sem.at[k])
+            first = lax.div(z * (sig // groups), 128) * 128
+            last = sig + z * (conv // groups)
+            outs = [(f, first, sig_out, k), (f, last, conv_out, 4 * groups + k)]
         else:
-            copy = pltpu.make_async_copy(g.at[block, :], g_out.at[block, :], out_sem.at[groups + k])
-        copy.start()
-        written.append(copy)
+            outs = [(g, z * (kv // groups), g_out, groups + k)]
+        for here, column, there, at in outs:
+            cols = pl.ds(pl.multiple_of(column, 128), there.shape[1])
+            copy = pltpu.make_async_copy(
+                here.at[block, cols], there.at[block, :], out_sem.at[at]
+            )
+            copy.start()
+            written.append(copy)
 
     put(True, 0)
     for copy in weights:
@@ -457,6 +465,11 @@
         copy.wait()
 
 
+def sig_window(width, groups):
+    reach = max(q * width % 128 + width for q in range(groups))
+    return -(-reach // 128) * 128
+
+
 def gather_and_project(sig_x, conv_x, sig_w, conv_w, kv_w, kv_grad, select, line_part, line_sq):
     groups = lax.axis_size("dp")
     rows, sig = sig_x.shape
@@ -471,15 +484,16 @@
     return pl.pallas_call(
         functools.partial(gather_kernel, groups),
         out_shape=(
-            jax.ShapeDtypeStruct((everything, sig + conv), half),
-            jax.ShapeDtypeStruct((everything, kv), half),
+            jax.ShapeDtypeStruct((everything, sig_window(sig // groups, groups)), half),
+            jax.ShapeDtypeStruct((everything, conv // groups), half),
+            jax.ShapeDtypeStruct((everything, kv // groups), half),
             jax.ShapeDtypeStruct((everything, share), half),
             jax.ShapeDtypeStruct((everything, share), half),
             jax.ShapeDtypeStruct((8, everything), jnp.float32),
             jax.ShapeDtypeStruct((8, kv // groups), jnp.float32),
         ),
         in_specs=[hbm, hbm, hbm, hbm, hbm, hbm, vmem, vmem, vmem],
-        out_specs=(hbm, hbm, hbm, hbm, vmem, vmem),
+        out_specs=(hbm, hbm, hbm, hbm, hbm, vmem, vmem),
         scratch_shapes=[
             pltpu.VMEM((everything, sig + conv), half),
             pltpu.VMEM((everything, kv), half),
@@ -500,7 +514,7 @@
             dma((2 * groups,)),
             dma((2 * groups, 9)),
             dma((2 * groups, 9)),
-            dma((4 * groups,)),
+            dma((5 * groups,)),
             dma((groups, 8)),
             dma((groups, 8)),
             dma((groups,)),
@@ -530,7 +544,6 @@
     per_device = dest_rank.shape[0] // groups
     capacity = 2 * per_device // groups
     row_count, sig = siglip_features.shape
-    conv = convnext_features.shape[1]
     tile_rows = row_count // per_device
     kv = key_value_grad.shape[1]
 
@@ -557,7 +570,7 @@
     )
     line_vector = newline_embed.astype(jnp.float32)
     line_square = jnp.sum(line_vector * line_vector)
-    features, grads, projected, normed_grad, stats, line_total = gather_and_project(
+    sig_cols, conv_cols, grads, projected, normed_grad, stats, line_total = gather_and_project(
         siglip_features,
         convnext_features,
         siglip_projection,
@@ -568,6 +581,8 @@
         line_part,
         jnp.full((8, row_count), line_square),
     )
+    width = sig // groups
+    sig_cols = lax.dynamic_slice_in_dim(sig_cols, lax.rem(my_rank * width, 128), width, 1)
     squares, products, line_square = stats[0], stats[1], stats[2, 0]
     line_total = line_total[0]
 
@@ -580,15 +595,12 @@
         inverse * grad_values - inverse**3 * proj_values * products[:, None] / D
     ).astype(jnp.bfloat16)
 
-    def block(x, first, width):
-        return lax.dynamic_slice_in_dim(x, first + my_rank * (width // groups), width // groups, 1)
-
     def contract(a, b):
         return lax.dot_general(a, b, (((0,), (0,)), ((), ())), preferred_element_type=jnp.float32)
 
-    siglip_result = contract(block(features, 0, sig), projected_grad)
-    convnext_result = contract(block(features, sig, conv), projected_grad)
-    kv_result = contract(block(grads, 0, kv), normed)
+    siglip_result = contract(sig_cols, projected_grad)
+    convnext_result = contract(conv_cols, projected_grad)
+    kv_result = contract(grads, normed)
     kv_result = kv_result + line_total[:, None] * line_normed.astype(jnp.float32)[None, :]
     return (siglip_result, convnext_result, kv_result)
 

time: 157 us -> 151 us (0.962)
  matrix products: 19.3 us -> 13.8 us
    dot_general x3, matrix products: 18.3 us -> 12.8 us  [contract(): lax.dot_general(a, b, (((0,), (0,)), ((), ())), preferred_element_type=jn...]
where the time goes in v5:
time: 151 us; the launch traced here: 150 us
  Pallas kernels  121 us (80%)
  matrix products  13.8 us (9%)
  other arithmetic  9.51 us (6%)
  local copies, waits for them, and re-layouts  4.58 us (3%)
    pallas_call x1, Pallas kernels, gather_and_project(): pl.pallas_call(functools.partial(gather_kernel, groups), out_shape=(jax.S...  121 us
    dot_general x3, matrix products, contract(): lax.dot_general(a, b, (((0,), (0,)), ((), ())), preferred_element_type=jn...  12.8 us

profile of v5, /device:TPU:0, one launch (start us, length us, event | category | flops | bytes accessed | tf_op | source)
XLA Modules:
  0.0 150.1 jit_solution(14266194113441877036)
XLA Ops:
  0.6 1.3 fusion.18
  1.9 0.5 broadcast.94
  2.4 1.3 reduce.3
  3.8 0.7 bitcast_and_fusion
  4.4 0.1 eq.55
  4.5 1.3 broadcast_in_dim.5.line_sq
  5.8 0.1 fusion.16
  5.9 0.2 select_reduce_fusion
  6.1 0.1 reshape.98
  6.2 0.7 fusion.24
  6.9 0.1 convert_reduce_fusion
  7.1 1.0 fusion.13
  8.1 0.1 iota_add_fusion
  8.2 0.1 add.68
  8.3 0.6 broadcast_in_dim.4.line_part
  8.9 1.2 fusion.8.select
  10.1 0.0 copy-start.2
  10.1 120.8 %shard_map.121 = (bf16[2048,384]{1,0:T(8,128)(2,1)}, bf16[2048,384]{1,0:T(8,128)(2,1)}, bf16[2048,512]{1,0:T(8,128)(2,1)}, bf16[2048,1024]{1,0:T(8,128)(2,1)}, b...) custom-call(bf16[512,1152]{1,0:T(8,128)(2,1)} %sig_ref.1, bf16[512,1536]{1,0:T(8,128)(2,1)} %conv_ref.1, ...), custom_call_target="tpu_custom_call" | custom-call | tf_op jit(solution)/shard_map/pallas_call | solution.py:484
  130.9 1.2 slice.15
  132.8 0.7 slice.14
  133.5 0.0 copy-done.2
  133.5 0.9 add_rsqrt_fusion
  134.4 0.0 copy-start
  134.5 0.0 copy-start.1
  134.5 6.8 %multiply_add_fusion = f32[512,1024]{1,0:T(8,128)} fusion(bf16[2048,512]{1,0:T(8,128)(2,1)} %get-tuple-element.15, bf16[2048,1024]{1,0:T(8,128)(2,1)} %get-tuple-element.13, f32[2048]{0:T(1024)S(1)} %bitcast.27, f32[1024]{0:T(1024)S(1)} %fusion.20, f32[512]{0:T(512)S(1)} %bitcast.32), kind=kOutput, calls=%fused_computation.9 | convolution fusion | flops 2154823680 | bytes 8402944 | tf_op jit(solution)/shard_map/dot_general | solution.py:599
  141.2 0.0 copy-done
  141.2 0.0 copy-done.1
  141.2 0.0 copy-start.4
  141.2 2.8 %fusion.3 = bf16[2048,1024]{1,0:T(8,128)(2,1)S(1)} fusion(bf16[2048,1024]{1,0:T(8,128)(2,1)S(1)} %copy-done, bf16[2048,1024]{1,0:T(8,128)(2,1)S(1)} %copy-done.1, f32[2048]{0:T(1024)S(1)} %bitcast.31, f32[2048]{0:T(1024)S(1)} %multiply_multiply_fusion, f32[2048]{0:T(1024)S(1)} %bitcast.29), kind=kLoop, calls=%fused_computation.5 | loop fusion | flops 16777216 | bytes 12607488 | tf_op jit(solution)/shard_map/convert_element_type | solution.py:596
  144.1 0.0 copy-done.4
  144.1 0.0 copy-start.3
  144.1 3.1 %fusion.9 = f32[288,1024]{1,0:T(8,128)} fusion(bf16[2048,1024]{1,0:T(8,128)(2,1)S(1)} %fusion.3, bf16[2048,384]{1,0:T(8,128)(2,1)S(1)} %copy-done.4, s32[]{:T(128)S(6)} %select_n.18), kind=kOutput, calls=%fused_computation.12 | convolution fusion | flops 1207959552 | bytes 6946820 | tf_op jit(solution)/shard_map/dot_general | solution.py:599
  147.1 0.0 copy-done.3
  147.1 3.0 %fusion.27 = f32[384,1024]{1,0:T(8,128)} fusion(bf16[2048,384]{1,0:T(8,128)(2,1)S(1)} %copy-done.3, bf16[2048,1024]{1,0:T(8,128)(2,1)S(1)} %fusion.3), kind=kOutput, calls=%fused_computation.44 | convolution fusion | flops 1610612736 | bytes 7340032 | tf_op jit(solution)/shard_map/dot_general | solution.py:599
  (5 shorter events, 0.1 us)
Async XLA Ops:
  10.1 123.4 %copy-start.2 = (bf16[1024]{0:T(1024)(128)(2,1)S(1)}, bf16[1024]{0:T(1024)(128)(2,1)}, u32[]{:S(2)}) copy-start(bf16[1024]{0:T(1024)(128)(2,1)} %param.14) | copy-start | bytes 6148
  134.4 6.8 %copy-start = (bf16[2048,1024]{1,0:T(8,128)(2,1)S(1)}, bf16[2048,1024]{1,0:T(8,128)(2,1)}, u32[]{:S(2)}) copy-start(bf16[2048,1024]{1,0:T(8,128)(2,1)} %get-tuple-element.13) | copy-start | bytes 12582916
  134.5 6.8 %copy-start.1 = (bf16[2048,1024]{1,0:T(8,128)(2,1)S(1)}, bf16[2048,1024]{1,0:T(8,128)(2,1)}, u32[]{:S(2)}) copy-start(bf16[2048,1024]{1,0:T(8,128)(2,1)} %get-tuple-element.12) | copy-start | bytes 12582916
  141.2 2.8 %copy-start.4 = (bf16[2048,384]{1,0:T(8,128)(2,1)S(1)}, bf16[2048,384]{1,0:T(8,128)(2,1)}, u32[]{:S(2)}) copy-start(bf16[2048,384]{1,0:T(8,128)(2,1)} %get-tuple-element.10) | copy-start | bytes 4718596
  144.1 3.1 %copy-start.3 = (bf16[2048,384]{1,0:T(8,128)(2,1)S(1)}, bf16[2048,384]{1,0:T(8,128)(2,1)}, u32[]{:S(2)}) copy-start(bf16[2048,384]{1,0:T(8,128)(2,1)} %get-tuple-element.14) | copy-start | bytes 4718596
